TPU v7x, 32 devices: a whole 2x2x4 slice. The times are simulated.
32 devices in a mesh: ctx: 2 (over x), exp: 16 (over z, y, core).
Axes of the slice: x: 2, y: 2, z: 4, core: 2. Of those that a mesh axis runs over, the one named last changes fastest.
Arguments:
- queries: bfloat16 [4096, 3072], P('ctx', 'exp'), may hold values from -16 to 16, as said below
- latent: bfloat16 [4096, 576], P('ctx'), may hold values from -6 to 6, as said below
- key_up_weight: bfloat16 [16, 128, 512], P('exp'), may hold values from -0.5 to 0.5
- value_up_weight: bfloat16 [16, 512, 128], P('exp'), may hold values from -1 to 1
- block_order: int32 [16], replicated, may hold values from 0 to 15, each once
- expert_ids: int32 [4096, 8], P(('ctx', 'exp')), may hold values from 0 to 95, as said below
- gates: float32 [4096, 8], P(('ctx', 'exp')), may hold values from 0.05 to 1
- expert_rows: bfloat16 [2, 16, 2, 16, 36, 7168], P('ctx', 'exp'), may hold values from -6 to 6
Outputs:
- attended: bfloat16 [4096, 2048], P('ctx', 'exp')
- combined: bfloat16 [4096, 7168], P(('ctx', 'exp'))
Inputs may be any that keep to these rules, and one draw needn't show every extreme that they name: `queries`: queries with their rotary parts already applied. Normed latent and rotary key, rotary parts already applied. `expert_ids`: each row names 8 different experts; expert e belongs to device e // 3. Among the rows of one device's 128 tokens at most 36 pairs name experts of one owning device, and some owning device receives exactly 36 from every device. `block_order`: each of the 16 sequence blocks appears once.
All inputs are finite; a program needn't handle non-finite values.
Results may differ from a plain program's by a relative error of at most 0.0084.
Values may be sent and summed in bfloat16 or wider, within the bound.
No kernel may reach another device: no remote copies, remote signals or barrier semaphores. Data moves between devices by JAX's collectives and lax.ppermute only.
A program may use at most 256 MiB of HBM per device.

v0:
```python
import math

import jax
import jax.numpy as jnp
from jax import lax
from jax.sharding import PartitionSpec as P

LATENT_WIDTH = 512
PLAIN_HEAD_WIDTH = 128
ROTARY_WIDTH = 64
VALUE_WIDTH = 128
EXP_DEV = 3


ROUTE_SCALE = 2.827


def lookup(block_order, row_ids, block_len):
    block_index = row_ids // block_len
    block_ids = jnp.arange(block_order.shape[0], dtype=jnp.int32)
    starts = jnp.sum(
        jnp.where(block_index[:, None] == block_ids[None, :], block_order[None, :], 0), axis=1
    )
    return starts * block_len + row_ids % block_len


def slot_numbers(owners, devices):
    flat_owners = owners.reshape(-1)
    onehot = (flat_owners[:, None] == jnp.arange(devices, dtype=jnp.int32)[None, :]).astype(
        jnp.int32
    )
    before = jnp.cumsum(onehot, axis=0) - onehot
    return jnp.sum(before * onehot, axis=1).reshape(owners.shape)


def shards(
    queries, latent, key_up_weight, value_up_weight, block_order, expert_ids, gates, expert_rows
):
    local_len = queries.shape[0]
    block_len = local_len // (block_order.shape[0] // lax.axis_size("ctx"))
    head_count = key_up_weight.shape[0]
    ctx_place = lax.axis_index("ctx")
    query_pos = lookup(
        block_order, ctx_place * local_len + jnp.arange(local_len, dtype=jnp.int32), block_len
    )
    score_scale = 1.0 / math.sqrt(PLAIN_HEAD_WIDTH + ROTARY_WIDTH)
    per_head = queries.reshape(local_len, head_count, PLAIN_HEAD_WIDTH + ROTARY_WIDTH)
    q_latent = jnp.einsum(
        "thn,hnc->thc",
        per_head[:, :, :PLAIN_HEAD_WIDTH],
        key_up_weight,
        preferred_element_type=jnp.float32,
    ).astype(jnp.bfloat16)
    query_full = jnp.concatenate([q_latent, per_head[:, :, PLAIN_HEAD_WIDTH:]], axis=2)
    key_segment = lax.all_gather(latent, "ctx", axis=0, tiled=True)
    key_rows = jnp.arange(key_segment.shape[0], dtype=jnp.int32)
    key_pos = lookup(block_order, key_rows, block_len)
    row_max = jnp.full((head_count, local_len), -1e30, jnp.float32)
    allowed = (key_pos[None, :] <= query_pos[:, None])[None]
    scores = (
        jnp.einsum("thc,sc->hts", query_full, key_segment, preferred_element_type=jnp.float32)
        * score_scale
    )
    masked = jnp.where(allowed, scores, -1e30)
    new_max = jnp.maximum(row_max, jnp.max(masked, axis=2))
    attention_probabilities = jnp.where(allowed, jnp.exp(masked - new_max[:, :, None]), 0.0)
    weight_sum = jnp.sum(attention_probabilities, axis=2)
    weighted = jnp.einsum(
        "hts,sc->htc",
        attention_probabilities.astype(jnp.bfloat16),
        key_segment[:, :LATENT_WIDTH],
        preferred_element_type=jnp.float32,
    )
    row_max, weight_sum, weighted = (new_max, weight_sum, weighted)
    latent_out = (weighted / weight_sum[:, :, None]).astype(jnp.bfloat16)
    attended = jnp.einsum(
        "htc,hcv->thv", latent_out, value_up_weight, preferred_element_type=jnp.float32
    ).astype(jnp.bfloat16)
    attended = attended.reshape(local_len, head_count * VALUE_WIDTH)
    devices = lax.axis_size("ctx") * lax.axis_size("exp")
    capacity = expert_rows.shape[4]
    model_width = expert_rows.shape[5]
    owners = expert_ids // EXP_DEV
    slots = slot_numbers(owners, devices)
    exchanged = lax.all_to_all(
        expert_rows.reshape(devices, capacity, model_width),
        ("ctx", "exp"),
        split_axis=0,
        concat_axis=0,
        tiled=True,
    )
    returned = exchanged.reshape(devices * capacity, model_width)
    scaled_gates = ROUTE_SCALE * gates / jnp.sum(gates, axis=1, keepdims=True)
    running = jnp.zeros((expert_ids.shape[0], model_width), jnp.float32)
    for k in range(expert_ids.shape[1]):
        picked = jnp.take(returned, owners[:, k] * capacity + slots[:, k], axis=0)
        running = running + scaled_gates[:, k : k + 1] * picked.astype(jnp.float32)
    combined = running.astype(jnp.bfloat16)
    return (attended, combined)


def solution(mesh):
    return jax.shard_map(
        shards,
        mesh=mesh,
        in_specs=(
            P("ctx", "exp"),
            P("ctx", None),
            P("exp", None, None),
            P("exp", None, None),
            P(),
            P(("ctx", "exp"), None),
            P(("ctx", "exp"), None),
            P("ctx", "exp", None, None, None, None),
        ),
        out_specs=(P("ctx", "exp"), P(("ctx", "exp"), None)),
        check_vma=False,
    )
```

profile of v0, /device:TPU:3, one launch (start us, length us, event | category | flops | bytes accessed | tf_op | source)
XLA Modules:
  0.0 588.5 jit_solution(2839429082619813091)
XLA Ops:
  7.2 8.4 %copy.55 = bf16[1,1,2,16,36,7168]{5,3,2,4,1,0:T(8,128)(2,1)S(1)} copy(bf16[1,1,2,16,36,7168]{5,3,4,2,1,0:T(8,128)(2,1)} %param.17) | data formatting | bytes 33030144 | tf_op args[7]
  15.6 25.1 %copy.56 = bf16[32,36,7168]{2,1,0:T(8,128)(2,1)} copy(bf16[32,36,7168]{2,0,1:T(8,128)(2,1)S(1)} %bitcast.107) | data formatting | bytes 33030144 | tf_op jit(solution)/shard_map/reshape | solution.py:86
  40.7 6.5 %all-to-all-start = ((bf16[32,36,7168]{2,1,0:T(8,128)(2,1)}), bf16[32,36,7168]{2,1,0:T(8,128)(2,1)}, u32[]{:S(2)}, u32[]{:S(2)}) async-start(bf16[32,36,7168]{2,1,0:T(8,128)(2,1)} %copy.56), calls=%async_computation | async-start | bytes 36700160 | tf_op jit(solution)/shard_map/all_to_all | solution.py:85
  47.3 0.7 all-gather.2.cloned.1.call-update
  48.4 9.0 %reduce-window.6 = s32[32,8,128]{2,1,0:T(8,128)S(1)} reduce-window(s32[32,8,128]{2,1,0:T(8,128)S(1)} %fusion.24, s32[]{:T(128)} %constant.80.clone.1), window={size=1x1x128 pad=0_0x0_0x127_0}, to_apply=%region_5.6 | reduce-window | flops 4161536 | bytes 262148 | tf_op jit(solution)/shard_map/reduce-window
  57.5 0.1 copy.52
  58.0 0.2 fusion.47
  59.1 0.1 select_reduce_fusion
  59.2 0.7 fusion.7
  60.0 197.2 %all-gather.2.cloned.1.call-done = bf16[4096,576]{0,1:T(8,128)(2,1)} async-done(((bf16[2048,576]{0,1:T(8,128)(2,1)}), bf16[4096,576]{0,1:T(8,128)(2,1)}) %all-gather.2.cloned.1.call-update) | async-done | bytes 4718608 | tf_op jit(solution)/shard_map/all_gather | solution.py:55
  257.2 23.0 %fusion = (f32[2048]{0:T(1024)S(1)}, f32[2048,4096]{1,0:T(8,128)}) fusion(s32[4096]{0:T(1024)S(1)} %fusion.31, s32[2048]{0:T(1024)S(1)} %fusion.33, bf16[4096,576]{0,1:T(8,128)(2,1)} %all-gather.2.cloned.1.call-done, bf16[2048,1,64]{0,2,1:T(8,128)(2,1)S(1)} %slice.133, bf16[2048,1,512]{0,2,1:T(8,128)(2,1)S(1)} %fusion.7), kind=kOutput, calls=%fused_computation.10 | convolution fusion | flops 9701947392 | bytes 40665088 | tf_op jit(solution)/shard_map/thc,sc->hts/dot_general | solution.py:61
  280.2 15.6 %fusion.1 = f32[2048]{0:T(1024)S(1)} fusion(f32[2048,4096]{1,0:T(8,128)} %get-tuple-element.50, f32[2048]{0:T(1024)S(1)} %broadcast_maximum_fusion, s32[4096]{0:T(1024)S(1)} %fusion.31, s32[2048]{0:T(1024)S(1)} %fusion.33), kind=kLoop, calls=%fused_computation.11 | loop fusion | flops 50329600 | bytes 33595392 | tf_op jit(solution)/shard_map/reduce_sum | solution.py:67
  295.8 19.6 %convolution_convert_fusion.1 = bf16[2048,128]{1,0:T(8,128)(2,1)} fusion(f32[2048]{0:T(1024)S(1)} %fusion.1, f32[2048,4096]{1,0:T(8,128)} %get-tuple-element.50, f32[2048]{0:T(1024)S(1)} %broadcast_maximum_fusion, s32[4096]{0:T(1024)S(1)} %fusion.31, s32[2048]{0:T(1024)S(1)} %fusion.33, bf16[4096,576]{0,1:T(8,128)(2,1)} %all-gather.2.cloned.1.call-done, ...), kind=kOutput, calls=%fused_computation.20 | convolution fusion | flops 8911060992 | bytes 38445056 | tf_op jit(solution)/shard_map/htc,hcv->thv/dot_general | solution.py:76
  315.4 129.8 %all-to-all-done = bf16[32,36,7168]{2,1,0:T(8,128)(2,1)} async-done(((bf16[32,36,7168]{2,1,0:T(8,128)(2,1)}), bf16[32,36,7168]{2,1,0:T(8,128)(2,1)}, u32[]{:S(2)}, u32[]{:S(2)}) %all-to-all-start) | async-done | bytes 16515104 | tf_op jit(solution)/shard_map/all_to_all | solution.py:85
  445.3 18.8 %reshape.218 = bf16[1152,7168]{1,0:T(8,128)(2,1)} reshape(bf16[32,36,7168]{2,1,0:T(8,128)(2,1)} %all-to-all-done) | data formatting | bytes 33030144 | tf_op jit(solution)/shard_map/reshape | solution.py:92
  464.1 11.2 %gather_fusion.7 = bf16[128,7168]{1,0:T(8,128)(2,1)S(1)} fusion(bf16[1152,7168]{1,0:T(8,128)(2,1)} %reshape.218, s32[1024]{0:T(1024)S(1)} %get-tuple-element.51), kind=kCustom, calls=%fused_computation.7.clone | custom fusion | bytes 3670528 | tf_op jit(solution)/shard_map/jit(_take)/gather | solution.py:96
  475.3 12.4 %gather_fusion.6 = bf16[128,7168]{1,0:T(8,128)(2,1)} fusion(bf16[1152,7168]{1,0:T(8,128)(2,1)} %reshape.218, s32[1024]{0:T(1024)S(1)} %get-tuple-element.52), kind=kCustom, calls=%fused_computation.6.clone | custom fusion | bytes 3670528 | tf_op jit(solution)/shard_map/jit(_take)/gather | solution.py:96
  487.7 21.2 %gather_fusion.5 = bf16[128,7168]{1,0:T(8,128)(2,1)} fusion(bf16[1152,7168]{1,0:T(8,128)(2,1)} %reshape.218, s32[1024]{0:T(1024)S(1)} %get-tuple-element.53), kind=kCustom, calls=%fused_computation.5.clone | custom fusion | bytes 3670528 | tf_op jit(solution)/shard_map/jit(_take)/gather | solution.py:96
  508.9 12.4 %gather_fusion.4 = bf16[128,7168]{1,0:T(8,128)(2,1)} fusion(bf16[1152,7168]{1,0:T(8,128)(2,1)} %reshape.218, s32[1024]{0:T(1024)S(1)} %get-tuple-element.54), kind=kCustom, calls=%fused_computation.4.clone | custom fusion | bytes 3670528 | tf_op jit(solution)/shard_map/jit(_take)/gather | solution.py:96
  521.3 12.7 %gather_fusion.3 = bf16[128,7168]{1,0:T(8,128)(2,1)} fusion(bf16[1152,7168]{1,0:T(8,128)(2,1)} %reshape.218, s32[1024]{0:T(1024)S(1)} %get-tuple-element.55), kind=kCustom, calls=%fused_computation.3.clone | custom fusion | bytes 3670528 | tf_op jit(solution)/shard_map/jit(_take)/gather | solution.py:96
  533.9 12.5 %gather_fusion.2 = bf16[128,7168]{1,0:T(8,128)(2,1)} fusion(bf16[1152,7168]{1,0:T(8,128)(2,1)} %reshape.218, s32[1024]{0:T(1024)S(1)} %get-tuple-element.56), kind=kCustom, calls=%fused_computation.2.clone | custom fusion | bytes 3670528 | tf_op jit(solution)/shard_map/jit(_take)/gather | solution.py:96
  546.4 12.7 %gather_fusion.1 = bf16[128,7168]{1,0:T(8,128)(2,1)} fusion(bf16[1152,7168]{1,0:T(8,128)(2,1)} %reshape.218, s32[1024]{0:T(1024)S(1)} %get-tuple-element.57), kind=kCustom, calls=%fused_computation.1.clone | custom fusion | bytes 3670528 | tf_op jit(solution)/shard_map/jit(_take)/gather | solution.py:96
  559.2 12.5 %gather_fusion = bf16[128,7168]{1,0:T(8,128)(2,1)} fusion(bf16[1152,7168]{1,0:T(8,128)(2,1)} %reshape.218, s32[1024]{0:T(1024)S(1)} %get-tuple-element.58), kind=kCustom, calls=%fused_computation.clone | custom fusion | bytes 3670528 | tf_op jit(solution)/shard_map/jit(_take)/gather | solution.py:96
  571.6 9.6 %add_convert_fusion = bf16[128,7168]{1,0:T(8,128)(2,1)} fusion(bf16[128,7168]{1,0:T(8,128)(2,1)S(1)} %gather_fusion.7, bf16[128,7168]{1,0:T(8,128)(2,1)} %gather_fusion.6, bf16[128,7168]{1,0:T(8,128)(2,1)} %gather_fusion.5, bf16[128,7168]{1,0:T(8,128)(2,1)} %gather_fusion.4, bf16[128,7168]{1,0:T(8,128)(2,1)} %gather_fusion.3, ...), kind=kLoop, calls=%fused_computation.17 | loop fusion | flops 29360128 | bytes 16520192 | tf_op jit(solution)/shard_map/convert_element_type | solution.py:98
  (50 shorter events, 1.7 us)
Async XLA Ops:
  7.2 52.0 %copy-start = (bf16[1,128,512]{2,1,0:T(8,128)(2,1)S(1)}, bf16[1,128,512]{2,1,0:T(8,128)(2,1)}, u32[]{:S(2)}) copy-start(bf16[1,128,512]{2,1,0:T(8,128)(2,1)} %param.12) | copy-start | bytes 393220
  40.7 7.3 %copy-start.4 = (s32[128,8]{0,1:T(8,128)S(1)}, s32[128,8]{0,1:T(8,128)}, u32[]{:S(2)}) copy-start(s32[128,8]{0,1:T(8,128)} %param.15) | copy-start | bytes 12292
  40.7 7.6 %copy-start.2 = (bf16[2048,192]{0,1:T(8,128)(2,1)S(1)}, bf16[2048,192]{0,1:T(8,128)(2,1)}, u32[]{:S(2)}) copy-start(bf16[2048,192]{0,1:T(8,128)(2,1)} %param.10) | copy-start | bytes 2359300
  40.7 404.5 %all-to-all-start = ((bf16[32,36,7168]{2,1,0:T(8,128)(2,1)}), bf16[32,36,7168]{2,1,0:T(8,128)(2,1)}, u32[]{:S(2)}, u32[]{:S(2)}) async-start(bf16[32,36,7168]{2,1,0:T(8,128)(2,1)} %copy.56), calls=%async_computation | async-start | bytes 36700160 | tf_op jit(solution)/shard_map/all_to_all | solution.py:85
  47.2 11.6 %copy-start.3 = (f32[128,8]{0,1:T(8,128)S(1)}, f32[128,8]{0,1:T(8,128)}, u32[]{:S(2)}) copy-start(f32[128,8]{0,1:T(8,128)} %param.16) | copy-start | bytes 12292
  47.2 11.7 %copy-start.5 = (s32[16]{0:T(128)S(1)}, s32[16]{0:T(128)}, u32[]{:S(2)}) copy-start(s32[16]{0:T(128)} %param.14) | copy-start | bytes 196
  47.2 209.9 %all-gather.2.cloned.1.call-start = ((), (), s32[]{:S(2)}) async-start(), calls=%async_computation.1 | async-start | bytes 7077888 | tf_op jit(solution)/shard_map/all_gather | solution.py:55
  280.2 15.6 %copy-start.6 = (bf16[1,512,128]{2,1,0:T(8,128)(2,1)S(1)}, bf16[1,512,128]{2,1,0:T(8,128)(2,1)}, u32[]{:S(2)}) copy-start(bf16[1,512,128]{2,1,0:T(8,128)(2,1)} %param.13) | copy-start | bytes 393220
  571.6 9.6 %copy-start.1 = (bf16[1,128,512]{2,1,0:T(8,128)(2,1)S(1)}, bf16[1,128,512]{2,1,0:T(8,128)(2,1)}, u32[]{:S(2)}) copy-start(bf16[1,128,512]{2,1,0:T(8,128)(2,1)} %param.12) | copy-start | bytes 393220
Sparse Core Ops, SparseCore 0:
  49.6 207.5 all-gather.1
where the time goes:
time: 599 us; the launch traced here: 588 us
  waiting for transfers between devices  328 us (55%)
  local copies, waits for them, and re-layouts  161 us (27%)
  matrix products  43.4 us (7%)
  other arithmetic  34.7 us (6%)
  between operations  14.7 us (2%)
  starting transfers between devices  6.53 us (1%)
    all_gather x1, waiting for transfers between devices, shards(): key_segment = lax.all_gather(latent, 'ctx', axis=0, tiled=True)  197 us
    all_to_all x1, waiting for transfers between devices, shards(): lax.all_to_all(expert_rows.reshape(devices, capacity, model_width), ('ctx...  130 us
    gather x8, local copies, waits for them, and re-layouts, shards(): picked = jnp.take(returned, owners[:, k] * capacity + slots[:, k], axis=0)  108 us
    reshape x1, local copies, waits for them, and re-layouts, shards(): expert_rows.reshape(devices, capacity, model_width)  25.1 us
    dot_general x1, matrix products, shards(): jnp.einsum('thc,sc->hts', query_full, key_segment, preferred_element_type...  23 us
    dot_general x1, matrix products, shards(): jnp.einsum('htc,hcv->thv', latent_out, value_up_weight, preferred_element...  19.6 us
    reshape x1, local copies, waits for them, and re-layouts, shards(): returned = exchanged.reshape(devices * capacity, model_width)  18.8 us
    reduce_sum x1, other arithmetic, shards(): weight_sum = jnp.sum(attention_probabilities, axis=2)  15.6 us
  transfers between devices with their start and end apart: 2, of which 2 were waited for; matrix products, arithmetic and copies ran while one was open for 12% of the time, Pallas kernels for 0%

commit v1 on v0

v1 whole, which is shorter than its diff:
```python
import functools
import math

import jax
import jax.numpy as jnp
from jax import lax
from jax.experimental import pallas as pl
from jax.experimental.pallas import tpu as pltpu
from jax.sharding import PartitionSpec as P

LATENT_WIDTH = 512
PLAIN_HEAD_WIDTH = 128
ROTARY_WIDTH = 64
VALUE_WIDTH = 128
EXP_DEV = 3
ROUTE_SCALE = 2.827
AXES = ("ctx", "exp")
VMEM_LIMIT = 48 * 1024 * 1024

CHUNKS = (
    (512, "x"),
    (512, "y"),
    (1024, "x"),
    (1024, "y"),
    (1024, "x"),
    (1024, "y"),
    (1024, "x"),
    (1024, "y"),
)


def exchange(value, mask, devices):
    return lax.ppermute(value, AXES, [(i, i ^ mask) for i in range(devices)])


def low_mask(index, masks):
    total = 0
    for place, mask in enumerate(reversed(masks)):
        if (index >> place) & 1:
            total ^= mask
    return total


def pack_kernel(count, me_ref, *refs):
    ins, outs = refs[: 4 * count], refs[4 * count :]
    for quarter in range(4):
        blocks = [ins[quarter * count + d][0] for d in range(count)]
        outs[quarter][...] = jnp.concatenate(blocks, axis=0)


def pack(me, rows, start, width, first, rest):
    devices, capacity, _ = rows.shape
    count = devices // 8
    tile = 512 if width % 512 == 0 and start % 512 == 0 else 256

    def place(quarter, d, g, j, me_ref):
        fixed = (quarter & 1) ^ (first if quarter & 2 else 0) ^ low_mask(d, rest[1:])
        return (me_ref[0] ^ fixed ^ (g * rest[0]), 0, start // tile + j)

    in_specs = [
        pl.BlockSpec((1, capacity, tile), functools.partial(place, quarter, d))
        for quarter in range(4)
        for d in range(count)
    ]
    shape = jax.ShapeDtypeStruct((2 * count * capacity, width), rows.dtype)
    return pl.pallas_call(
        functools.partial(pack_kernel, count),
        grid_spec=pltpu.PrefetchScalarGridSpec(
            num_scalar_prefetch=1,
            grid=(2, width // tile),
            in_specs=in_specs,
            out_specs=[pl.BlockSpec((count * capacity, tile), lambda g, j, me_ref: (g, j))] * 4,
        ),
        out_shape=[shape] * 4,
        compiler_params=pltpu.CompilerParams(vmem_limit_bytes=VMEM_LIMIT),
        cost_estimate=pl.CostEstimate(
            flops=0, bytes_accessed=4 * devices * capacity * width, transcendentals=0
        ),
        name="pack_rows",
    )(me, *([rows] * (4 * count)))


def weights_kernel(count, capacity, first, me_ref, routes_ref, out_ref):
    step = pl.program_id(0)
    tokens = routes_ref.shape[2]
    topk = routes_ref.shape[1] // 2
    ids = routes_ref[0, :topk, :]
    gates = routes_ref[0, topk:, :]
    scaled = ROUTE_SCALE * gates / jnp.sum(gates, axis=0, keepdims=True)
    before = lax.broadcasted_iota(jnp.int32, (tokens, tokens), 0) < lax.broadcasted_iota(
        jnp.int32, (tokens, tokens), 1
    )
    before = jnp.where(before, 1.0, 0.0).astype(jnp.bfloat16)
    row = lax.broadcasted_iota(jnp.int32, (count * capacity, tokens), 0)
    row = row - lax.rem(step, count) * capacity
    row = row.astype(jnp.float32)
    for source in range(4):
        owner = me_ref[0] ^ ((source & 1) ^ (first if source & 2 else 0))
        low = (owner * EXP_DEV).astype(jnp.float32)
        match = jnp.where((ids >= low) & (ids < low + EXP_DEV), 1.0, 0.0)
        per_token = jnp.broadcast_to(jnp.sum(match, axis=0, keepdims=True), match.shape)
        prior = jnp.dot(
            per_token.astype(jnp.bfloat16), before, preferred_element_type=jnp.float32
        )
        slot = prior[0:1, :]
        total = jnp.zeros((count * capacity, tokens), jnp.float32)
        for k in range(topk):
            weight = scaled[k : k + 1, :] * match[k : k + 1, :]
            total = total + jnp.where(row == slot, weight, 0.0)
            slot = slot + match[k : k + 1, :]
        out_ref[0, source, :, :] = total.T.astype(jnp.bfloat16)


def combine_weights(me, routes, capacity, first, rest):
    devices, lines, tokens = routes.shape
    count = devices // 8

    def place(i, me_ref):
        index = me_ref[0]
        for bit, mask in enumerate(reversed(rest)):
            index = index ^ (((i >> bit) & 1) * mask)
        return (index, 0, 0)

    return pl.pallas_call(
        functools.partial(weights_kernel, count, capacity, first),
        grid_spec=pltpu.PrefetchScalarGridSpec(
            num_scalar_prefetch=1,
            grid=(2 * count,),
            in_specs=[pl.BlockSpec((1, lines, tokens), place)],
            out_specs=pl.BlockSpec(
                (1, 4, tokens, count * capacity),
                lambda i, me_ref: (i // count, 0, lax.rem(i, count), 0),
            ),
        ),
        out_shape=jax.ShapeDtypeStruct(
            (2, 4, count * tokens, count * capacity), jnp.bfloat16
        ),
        compiler_params=pltpu.CompilerParams(vmem_limit_bytes=VMEM_LIMIT),
        name="combine_weights",
    )(me, routes)


def weigh(weights_ref, row_refs):
    total = None
    for source, ref in enumerate(row_refs):
        part = jnp.dot(weights_ref[0, source], ref[...], preferred_element_type=jnp.float32)
        total = part if total is None else total + part
    return total


def send_kernel(weights_ref, a, b, c, d, out_ref):
    out_ref[...] = weigh(weights_ref, (a, b, c, d)).astype(out_ref.dtype)


def keep_kernel(weights_ref, a, b, c, d, got_ref, keep_ref, send_ref):
    total = weigh(weights_ref, (a, b, c, d)) + got_ref[...].astype(jnp.float32)
    half = keep_ref.shape[0]
    keep_ref[...] = total[:half].astype(keep_ref.dtype)
    send_ref[...] = total[half:].astype(send_ref.dtype)


def matmul_call(weights, rows, got, group):
    _, sources, out_rows, depth = weights.shape
    width = rows[0].shape[1]
    tile = 512 if width % 512 == 0 else 256
    in_specs = [pl.BlockSpec((1, sources, out_rows, depth), lambda j: (group, 0, 0, 0))]
    in_specs += [pl.BlockSpec((depth, tile), lambda j: (group, j))] * 4
    whole = pl.BlockSpec((out_rows, tile), lambda j: (0, j))
    half = pl.BlockSpec((out_rows // 2, tile), lambda j: (0, j))
    if got is None:
        kernel, extra, out_specs = send_kernel, (), whole
        out_shape = jax.ShapeDtypeStruct((out_rows, width), jnp.bfloat16)
    else:
        kernel, extra, out_specs = keep_kernel, (got,), [half, half]
        out_shape = [jax.ShapeDtypeStruct((out_rows // 2, width), jnp.bfloat16)] * 2
        in_specs.append(whole)
    return pl.pallas_call(
        kernel,
        grid=(width // tile,),
        in_specs=in_specs,
        out_specs=out_specs,
        out_shape=out_shape,
        compiler_params=pltpu.CompilerParams(vmem_limit_bytes=VMEM_LIMIT),
        cost_estimate=pl.CostEstimate(
            flops=2 * sources * out_rows * depth * width,
            bytes_accessed=2 * width * (sources * depth + 2 * out_rows),
            transcendentals=0,
        ),
        name="partial_sums",
    )(weights, *rows, *extra)


def attention_kernel(
    scale, key_index, query_block, queries_ref, key_up_ref, value_up_ref, *refs
):
    blocks = len(refs) - 4
    keys, out_ref = refs[:blocks], refs[blocks]
    scores_ref, total_ref, weight_ref = refs[blocks + 1 :]
    block_len = queries_ref.shape[0]
    place = query_block[pl.program_id(0)]
    queries = queries_ref[...]
    absorbed = jnp.dot(
        queries[:, :PLAIN_HEAD_WIDTH], key_up_ref[...], preferred_element_type=jnp.float32
    ).astype(jnp.bfloat16)
    rotary = queries[:, PLAIN_HEAD_WIDTH:]
    contract = (((1,), (1,)), ((), ()))
    ahead = lax.broadcasted_iota(jnp.int32, (block_len, block_len), 1) > lax.broadcasted_iota(
        jnp.int32, (block_len, block_len), 0
    )

    def scores_of(j):
        plain = lax.dot_general(
            absorbed, keys[j][:, :LATENT_WIDTH], contract, preferred_element_type=jnp.float32
        )
        turned = lax.dot_general(
            rotary, keys[j][:, LATENT_WIDTH:], contract, preferred_element_type=jnp.float32
        )
        return (plain + turned) * scale

    total_ref[...] = jnp.full(total_ref.shape, -1e30, jnp.float32)
    lanes = total_ref.shape[1]

    def lane_max(values):
        best = total_ref[...]
        for i in range(block_len // lanes):
            best = jnp.maximum(best, values[:, i * lanes : (i + 1) * lanes])
        total_ref[...] = best

    for j in range(blocks):

        @pl.when(j < place)
        def _():
            scores = scores_of(j)
            scores_ref[j] = scores
            lane_max(scores)

        @pl.when(j == place)
        def _():
            scores = jnp.where(ahead, -1e30, scores_of(j))
            scores_ref[j] = scores
            lane_max(scores)

    row_max = jnp.max(total_ref[...], axis=1, keepdims=True)
    total_ref[...] = jnp.zeros(total_ref.shape, jnp.float32)
    weight_ref[...] = jnp.zeros(weight_ref.shape, jnp.float32)
    for j in range(blocks):

        @pl.when(j <= place)
        def _():
            probs = jnp.exp(scores_ref[j] - row_max)
            some = total_ref[...]
            for i in range(block_len // lanes):
                some = some + probs[:, i * lanes : (i + 1) * lanes]
            total_ref[...] = some
            weight_ref[...] += jnp.dot(
                probs.astype(jnp.bfloat16),
                keys[j][:, :LATENT_WIDTH],
                preferred_element_type=jnp.float32,
            )

    weight_sum = jnp.sum(total_ref[...], axis=1, keepdims=True)
    latent_out = (weight_ref[...] / weight_sum).astype(jnp.bfloat16)
    out_ref[...] = jnp.dot(
        latent_out, value_up_ref[...], preferred_element_type=jnp.float32
    ).astype(out_ref.dtype)


def attend(queries, keys, key_up, value_up, key_index, query_block, first, count):
    blocks = key_index.shape[0]
    block_len = keys.shape[0] // blocks
    head_width = queries.shape[1]

    def key_place(p, i, key_index, query_block):
        return (key_index[p], 0)

    in_specs = [
        pl.BlockSpec((block_len, head_width), lambda i, a, b: (first + i, 0)),
        pl.BlockSpec(key_up.shape, lambda i, a, b: (0, 0)),
        pl.BlockSpec(value_up.shape, lambda i, a, b: (0, 0)),
    ]
    in_specs += [
        pl.BlockSpec((block_len, keys.shape[1]), functools.partial(key_place, p))
        for p in range(blocks)
    ]
    scale = 1.0 / math.sqrt(PLAIN_HEAD_WIDTH + ROTARY_WIDTH)
    return pl.pallas_call(
        functools.partial(attention_kernel, scale),
        grid_spec=pltpu.PrefetchScalarGridSpec(
            num_scalar_prefetch=2,
            grid=(count,),
            in_specs=in_specs,
            out_specs=pl.BlockSpec((block_len, VALUE_WIDTH), lambda i, a, b: (i, 0)),
            scratch_shapes=[
                pltpu.VMEM((blocks, block_len, block_len), jnp.float32),
                pltpu.VMEM((block_len, 128), jnp.float32),
                pltpu.VMEM((block_len, LATENT_WIDTH), jnp.float32),
            ],
        ),
        out_shape=jax.ShapeDtypeStruct((count * block_len, VALUE_WIDTH), jnp.bfloat16),
        compiler_params=pltpu.CompilerParams(vmem_limit_bytes=VMEM_LIMIT),
        cost_estimate=pl.CostEstimate(
            flops=count * blocks * block_len * block_len * 1100,
            bytes_accessed=2 * keys.size,
            transcendentals=count * blocks * block_len * block_len // 2,
        ),
        name="latent_attention",
    )(key_index, query_block[first : first + count], queries, key_up, value_up, *([keys] * blocks))


def shards(
    queries, latent, key_up_weight, value_up_weight, block_order, expert_ids, gates, expert_rows
):
    n_ctx, n_exp = lax.axis_size("ctx"), lax.axis_size("exp")
    devices = n_ctx * n_exp
    ctx = lax.axis_index("ctx").astype(jnp.int32)
    exp = lax.axis_index("exp").astype(jnp.int32)
    me = (ctx * n_exp + exp).reshape(1)
    capacity, model_width = expert_rows.shape[4:]
    rows = expert_rows.reshape(devices, capacity, model_width)

    local_routes = jnp.concatenate([expert_ids.T.astype(jnp.float32), gates.T], axis=0)
    routes = lax.all_gather(local_routes, AXES, axis=0)

    local_len = latent.shape[0]
    eighth = local_len // 8
    mine = lax.dynamic_slice_in_dim(latent, (exp % 8) * eighth, eighth, axis=0)
    crossed = exchange(mine, n_exp, devices)
    groups = [list(range(i, i + 8)) for i in range(0, n_exp, 8)]
    other = lax.all_gather(crossed, "exp", axis=0, tiled=True, axis_index_groups=groups)
    keys = jnp.concatenate([latent, other], axis=0)

    extra = [1 << b for b in range(4, n_exp.bit_length() - 1)]
    orders = {"x": [n_exp, 2, 4, 8] + extra, "y": [2, n_exp, 4, 8] + extra}
    weights = {
        name: combine_weights(me, routes, capacity, order[0], order[1:])
        for name, order in orders.items()
    }
    pieces = []
    start = 0
    for width, name in CHUNKS:
        order = orders[name]
        first, rest = order[0], order[1:]
        packed = pack(me, rows, start, width, first, rest)
        start += width
        held = [packed[0]]
        for quarter, mask in ((1, 1), (2, first), (3, 1 ^ first)):
            held.append(exchange(packed[quarter], mask, devices))
        got = exchange(matmul_call(weights[name], held, None, 1), rest[0], devices)
        keep, send = matmul_call(weights[name], held, got, 0)
        for mask in rest[1:]:
            got = exchange(send, mask, devices)
            total = keep.astype(jnp.float32) + got.astype(jnp.float32)
            total = total.astype(jnp.bfloat16)
            half = total.shape[0] // 2
            keep, send = total[:half], total[half:]
        pieces.append(total)
    combined = jnp.concatenate(pieces, axis=1)

    blocks = block_order.shape[0]
    local_blocks = blocks // n_ctx
    ids = jnp.arange(blocks, dtype=jnp.int32)
    stored = jnp.sum(jnp.where(block_order[None, :] == ids[:, None], ids[None, :], 0), axis=1)
    key_index = ((stored // local_blocks) ^ ctx) * local_blocks + stored % local_blocks
    query_block = lax.dynamic_slice_in_dim(block_order, ctx * local_blocks, local_blocks)
    heads = key_up_weight.shape[0]
    head_width = PLAIN_HEAD_WIDTH + ROTARY_WIDTH
    per_call = 2
    columns = []
    for h in range(heads):
        head_queries = queries[:, h * head_width : (h + 1) * head_width]
        parts = [
            attend(
                head_queries, keys, key_up_weight[h], value_up_weight[h], key_index, query_block, b, per_call
            )
            for b in range(0, local_blocks, per_call)
        ]
        columns.append(jnp.concatenate(parts, axis=0))
    attended = columns[0] if heads == 1 else jnp.concatenate(columns, axis=1)
    return (attended, combined)


def solution(mesh):
    return jax.shard_map(
        shards,
        mesh=mesh,
        in_specs=(
            P("ctx", "exp"),
            P("ctx", None),
            P("exp", None, None),
            P("exp", None, None),
            P(),
            P(("ctx", "exp"), None),
            P(("ctx", "exp"), None),
            P("ctx", "exp", None, None, None, None),
        ),
        out_specs=(P("ctx", "exp"), P(("ctx", "exp"), None)),
        check_vma=False,
    )
```

time: 599 us -> 462 us (0.77)
  waiting for transfers between devices: 328 us -> 153 us
  Pallas kernels: 0 us -> 139 us
  local copies, waits for them, and re-layouts: 161 us -> 34.6 us
  blocking collectives: 0 us -> 61.5 us
  matrix products: 43.4 us -> 0 us
  starting transfers between devices: 6.53 us -> 36.2 us
  other arithmetic: 34.7 us -> 14.7 us
    all_gather x1, waiting for transfers between devices: 197 us -> 0.01 us  [shards(): lax.all_gather(crossed, 'exp', axis=0, tiled=True, axis_index_groups=groups)]
    ppermute x0 -> x49, waiting for transfers between devices: none -> 153 us  [exchange(): return lax.ppermute(value, AXES, [(i, i ^ mask) for i in range(devices)])]
    pallas_call x0 -> x30, Pallas kernels: none -> 139 us  [the longest x4 58.5 us: attend(): pl.pallas_call(functools.partial(attention_kernel, scale), grid_spec=pltp...]
    all_to_all x1 -> x0, waiting for transfers between devices: 130 us -> none  [shards(): lax.all_to_all(expert_rows.reshape(devices, capacity, model_width), ('ctx...]
    gather x8 -> x0, local copies, waits for them, and re-layouts: 108 us -> none  [shards(): picked = jnp.take(returned, owners[:, k] * capacity + slots[:, k], axis=0)]
    all_gather x0 -> x1, blocking collectives: none -> 61.5 us  [shards(): routes = lax.all_gather(local_routes, AXES, axis=0)]
    reshape x3 -> x0, local copies, waits for them, and re-layouts: 44 us -> none  [the longest x1 25.1 us: shards(): expert_rows.reshape(devices, capacity, model_width)]
    dot_general x3 -> x0, matrix products: 43.4 us -> none  [the longest x1 23 us: shards(): jnp.einsum('thc,sc->hts', query_full, key_segment, preferred_element_type...]
  transfers between devices with their start and end apart: 2 -> 50, of which waited for: 2 -> 20; matrix products, arithmetic and copies ran while one was open for 12% -> 6% of each run, Pallas kernels for 0% -> 18%
where the time goes in v1:
time: 462 us; the launch traced here: 454 us
  waiting for transfers between devices  153 us (33%)
  Pallas kernels  139 us (30%)
  blocking collectives  61.5 us (13%)
  starting transfers between devices  36.2 us (8%)
  local copies, waits for them, and re-layouts  34.6 us (7%)
  between operations  15.2 us (3%)
  other arithmetic  14.7 us (3%)
    ppermute x49, waiting for transfers between devices, exchange(): return lax.ppermute(value, AXES, [(i, i ^ mask) for i in range(devices)])  153 us
    all_gather x1, blocking collectives, shards(): routes = lax.all_gather(local_routes, AXES, axis=0)  61.5 us
    pallas_call x4, Pallas kernels, attend(): pl.pallas_call(functools.partial(attention_kernel, scale), grid_spec=pltp...  58.5 us
    pallas_call x16, Pallas kernels, matmul_call(): pl.pallas_call(kernel, grid=(width // tile,), in_specs=in_specs, out_spec...  45.8 us
    ppermute x49, starting transfers between devices, exchange(): return lax.ppermute(value, AXES, [(i, i ^ mask) for i in range(devices)])  36.2 us
    unnamed x135, local copies, waits for them, and re-layouts  33.5 us
    pallas_call x8, Pallas kernels, pack(): pl.pallas_call(functools.partial(pack_kernel, count), grid_spec=pltpu.Pre...  27.1 us
  transfers between devices with their start and end apart: 50, of which 20 were waited for; matrix products, arithmetic and copies ran while one was open for 6% of the time, Pallas kernels for 18%

profile of v1, /device:TPU:3, one launch (start us, length us, event | category | flops | bytes accessed | tf_op | source)
XLA Modules:
  0.0 454.4 jit_solution(13331058635492068407)
XLA Ops:
  11.2 18.2 %copy.23 = bf16[1,1,2,16,36,7168]{5,4,3,2,1,0:T(8,128)(2,1)} copy(bf16[1,1,2,16,36,7168]{5,3,4,2,1,0:T(8,128)(2,1)} %param.15) | data formatting | bytes 33030144 | tf_op args[7]
  37.0 4.0 pack_rows.10
  44.8 4.2 collective-permute-done.3.d
  59.5 5.0 %collective-permute-done.9.d = bf16[288,512]{1,0:T(8,128)(2,1)S(1)} collective-permute-done((bf16[288,512]{1,0:T(8,128)(2,1)S(1)}, bf16[288,512]{1,0:T(8,128)(2,1)S(1)}, u32[]{:S(2)}, u32[]{:S(2)}) %collective-permute-start.9) | collective-permute-done | bytes 294944 | tf_op jit(solution)/shard_map/ppermute | solution.py:33
  66.7 4.0 pack_rows.12
  86.4 7.2 %collective-permute-done.21.d = bf16[288,1024]{1,0:T(8,128)(2,1)} collective-permute-done((bf16[288,1024]{1,0:T(8,128)(2,1)}, bf16[288,1024]{1,0:T(8,128)(2,1)}, u32[]{:S(2)}, u32[]{:S(2)}) %collective-permute-start.21) | collective-permute-done | bytes 589856 | tf_op jit(solution)/shard_map/ppermute | solution.py:33
  95.5 61.5 %all-gather = f32[512,128]{1,0:T(8,128)S(1)} all-gather(f32[16,128]{1,0:T(8,128)S(1)} %pad_maximum_fusion.2), channel_id=2, replica_groups=mesh['ctx'=2,'exp'=16] {'ctx','exp'}, dimensions={0}, use_global_device_ids=true | all-gather | bytes 270336 | tf_op jit(solution)/shard_map/all_gather | solution.py:322
  186.7 6.0 %collective-permute-done.39.d = bf16[288,1024]{1,0:T(8,128)(2,1)} collective-permute-done((bf16[288,1024]{1,0:T(8,128)(2,1)}, bf16[288,1024]{1,0:T(8,128)(2,1)}, u32[]{:S(2)}, u32[]{:S(2)}) %collective-permute-start.39) | collective-permute-done | bytes 589856 | tf_op jit(solution)/shard_map/ppermute | solution.py:33
  194.5 8.3 %collective-permute-done.10.got_ref = bf16[512,512]{1,0:T(8,128)(2,1)} collective-permute-done((bf16[512,512]{1,0:T(8,128)(2,1)}, bf16[512,512]{1,0:T(8,128)(2,1)}, u32[]{:S(2)}, u32[]{:S(2)}) %collective-permute-start.10) | collective-permute-done | bytes 524320 | tf_op jit(solution)/shard_map/ppermute | solution.py:33
  221.3 8.7 %collective-permute-done.44.c = bf16[288,1024]{1,0:T(8,128)(2,1)S(1)} collective-permute-done((bf16[288,1024]{1,0:T(8,128)(2,1)}, bf16[288,1024]{1,0:T(8,128)(2,1)S(1)}, u32[]{:S(2)}, u32[]{:S(2)}) %collective-permute-start.44) | collective-permute-done | bytes 589856 | tf_op jit(solution)/shard_map/ppermute | solution.py:33
  230.0 13.2 %collective-permute-done.45.d = bf16[288,1024]{1,0:T(8,128)(2,1)S(1)} collective-permute-done((bf16[288,1024]{1,0:T(8,128)(2,1)}, bf16[288,1024]{1,0:T(8,128)(2,1)S(1)}, u32[]{:S(2)}, u32[]{:S(2)}) %collective-permute-start.45) | collective-permute-done | bytes 589856 | tf_op jit(solution)/shard_map/ppermute | solution.py:33
  269.1 8.0 %collective-permute-done.34.got_ref = bf16[512,1024]{1,0:T(8,128)(2,1)} collective-permute-done((bf16[512,1024]{1,0:T(8,128)(2,1)}, bf16[512,1024]{1,0:T(8,128)(2,1)}, u32[]{:S(2)}, u32[]{:S(2)}) %collective-permute-start.34) | collective-permute-done | bytes 1048608 | tf_op jit(solution)/shard_map/ppermute | solution.py:33
  280.2 7.3 %collective-permute-done.40.got_ref = bf16[512,1024]{1,0:T(8,128)(2,1)} collective-permute-done((bf16[512,1024]{1,0:T(8,128)(2,1)}, bf16[512,1024]{1,0:T(8,128)(2,1)}, u32[]{:S(2)}, u32[]{:S(2)}) %collective-permute-start.40) | collective-permute-done | bytes 1048608 | tf_op jit(solution)/shard_map/ppermute | solution.py:33
  290.7 8.9 %collective-permute-done.46.got_ref = bf16[512,1024]{1,0:T(8,128)(2,1)} collective-permute-done((bf16[512,1024]{1,0:T(8,128)(2,1)}, bf16[512,1024]{1,0:T(8,128)(2,1)}, u32[]{:S(2)}, u32[]{:S(2)}) %collective-permute-start.46) | collective-permute-done | bytes 1048608 | tf_op jit(solution)/shard_map/ppermute | solution.py:33
  309.8 24.4 %collective-permute-done.41 = bf16[256,1024]{1,0:T(8,128)(2,1)S(1)} collective-permute-done((bf16[256,1024]{1,0:T(8,128)(2,1)S(1)}, bf16[256,1024]{1,0:T(8,128)(2,1)S(1)}, u32[]{:S(2)}, u32[]{:S(2)}) %collective-permute-start.41) | collective-permute-done | bytes 524320 | tf_op jit(solution)/shard_map/ppermute | solution.py:33
  334.6 10.9 %collective-permute-done.47 = bf16[256,1024]{1,0:T(8,128)(2,1)S(1)} collective-permute-done((bf16[256,1024]{1,0:T(8,128)(2,1)S(1)}, bf16[256,1024]{1,0:T(8,128)(2,1)S(1)}, u32[]{:S(2)}, u32[]{:S(2)}) %collective-permute-start.47) | collective-permute-done | bytes 524320 | tf_op jit(solution)/shard_map/ppermute | solution.py:33
  350.5 20.1 %collective-permute-done.36 = bf16[128,1024]{1,0:T(8,128)(2,1)S(1)} collective-permute-done((bf16[128,1024]{1,0:T(8,128)(2,1)S(1)}, bf16[128,1024]{1,0:T(8,128)(2,1)S(1)}, u32[]{:S(2)}, u32[]{:S(2)}) %collective-permute-start.36) | collective-permute-done | bytes 262176 | tf_op jit(solution)/shard_map/ppermute | solution.py:33
  371.4 4.8 %collective-permute-done.42 = bf16[128,1024]{1,0:T(8,128)(2,1)S(1)} collective-permute-done((bf16[128,1024]{1,0:T(8,128)(2,1)S(1)}, bf16[128,1024]{1,0:T(8,128)(2,1)S(1)}, u32[]{:S(2)}, u32[]{:S(2)}) %collective-permute-start.42) | collective-permute-done | bytes 262176 | tf_op jit(solution)/shard_map/ppermute | solution.py:33
  377.0 4.8 %collective-permute-done.48 = bf16[128,1024]{1,0:T(8,128)(2,1)S(1)} collective-permute-done((bf16[128,1024]{1,0:T(8,128)(2,1)S(1)}, bf16[128,1024]{1,0:T(8,128)(2,1)S(1)}, u32[]{:S(2)}, u32[]{:S(2)}) %collective-permute-start.48) | collective-permute-done | bytes 262176 | tf_op jit(solution)/shard_map/ppermute | solution.py:33
  382.7 5.4 %pad_maximum_fusion.refs_0_.refs_1_.refs_2_.refs_3_.refs_4_.refs_5_.refs_6_.refs_7_.refs_8_.refs_9_.refs_10_.refs_11_.refs_12_.refs_13_.refs_14_.refs_15_ = bf16[4096,576]{1,0:T(8,128)(2,1)} fusion(bf16[2048,576]{1,0:T(8,128)(2,1)} %all-gather.3.cloned.1.call-done, bf16[2048,576]{1,0:T(8,128)(2,1)} %copy-done.55), kind=kLoop, calls=%fused_computation | loop fusion | flops 9437184 | bytes 9437184 | tf_op jit(solution)/shard_map/concatenate | solution.py:330
  388.0 18.7 %latent_attention.7 = bf16[512,128]{1,0:T(8,128)(2,1)S(1)} custom-call(s32[16]{0:T(128)S(1)} %fusion.8.key_index, s32[2]{0:T(128)S(1)} %get-tuple-element.99.query_block, bf16[2048,192]{1,0:T(8,128)(2,1)S(1)} %copy.19.queries_ref, bf16[128,512]{1,0:T(8,128)(2,1)S(1)} %bitcast.10, bf16[512,128]{1,0:T(8,128)(2,1)S(1)} %bitcast.14, ...), custom_call_target="tpu_custom_call" | custom-call | flops 2306867200 | bytes 4718592 | tf_op jit(solution)/shard_map/latent_attention/pallas_call | solution.py:286
  406.8 15.5 %latent_attention.6 = bf16[512,128]{1,0:T(8,128)(2,1)S(1)} custom-call(s32[16]{0:T(128)S(1)} %fusion.8.key_index, s32[2]{0:T(128)S(1)} %get-tuple-element.100.query_block, bf16[2048,192]{1,0:T(8,128)(2,1)S(1)} %copy.19.queries_ref, bf16[128,512]{1,0:T(8,128)(2,1)S(1)} %bitcast.11, bf16[512,128]{1,0:T(8,128)(2,1)S(1)} %bitcast.15, ...), custom_call_target="tpu_custom_call" | custom-call | flops 2306867200 | bytes 4718592 | tf_op jit(solution)/shard_map/latent_attention/pallas_call | solution.py:286
  422.3 8.3 %latent_attention.5 = bf16[512,128]{1,0:T(8,128)(2,1)S(1)} custom-call(s32[16]{0:T(128)S(1)} %fusion.8.key_index, s32[2]{0:T(128)S(1)} %get-tuple-element.101.query_block, bf16[2048,192]{1,0:T(8,128)(2,1)S(1)} %copy.19.queries_ref, bf16[128,512]{1,0:T(8,128)(2,1)S(1)} %bitcast.12, bf16[512,128]{1,0:T(8,128)(2,1)S(1)} %bitcast.16, ...), custom_call_target="tpu_custom_call" | custom-call | flops 2306867200 | bytes 4718592 | tf_op jit(solution)/shard_map/latent_attention/pallas_call | solution.py:286
  430.6 16.0 %latent_attention.4 = bf16[512,128]{1,0:T(8,128)(2,1)S(1)} custom-call(s32[16]{0:T(128)S(1)} %fusion.8.key_index, s32[2]{0:T(128)S(1)} %get-tuple-element.98.query_block, bf16[2048,192]{1,0:T(8,128)(2,1)S(1)} %copy.19.queries_ref, bf16[128,512]{1,0:T(8,128)(2,1)S(1)} %bitcast.13, bf16[512,128]{1,0:T(8,128)(2,1)S(1)} %bitcast.17, ...), custom_call_target="tpu_custom_call" | custom-call | flops 2306867200 | bytes 4718592 | tf_op jit(solution)/shard_map/latent_attention/pallas_call | solution.py:286
  (276 shorter events, 145.7 us)
Async XLA Ops:
  7.2 375.5 %all-gather.3.cloned.1.call-start = ((), (), s32[]{:S(2)}) async-start(), calls=%async_computation | async-start | bytes 2949120 | tf_op jit(solution)/shard_map/all_gather | solution.py:329
  42.8 31.4 %collective-permute-start.15 = (bf16[288,1024]{1,0:T(8,128)(2,1)}, bf16[288,1024]{1,0:T(8,128)(2,1)}, u32[]{:S(2)}, u32[]{:S(2)}) collective-permute-start(bf16[288,1024]{1,0:T(8,128)(2,1)} %get-tuple-element.65), channel_id=1, source_target_pairs={{0,17},{1,16},{2,19},{3,18},{4,21},{5,20},{6,23},{7,22},{8,25},{9,... | collective-permute-start | bytes 1769480 | tf_op jit(solution)/shard_map/ppermute | solution.py:33
  75.7 87.4 %collective-permute-start.27 = (bf16[288,1024]{1,0:T(8,128)(2,1)}, bf16[288,1024]{1,0:T(8,128)(2,1)}, u32[]{:S(2)}, u32[]{:S(2)}) collective-permute-start(bf16[288,1024]{1,0:T(8,128)(2,1)} %get-tuple-element.77), channel_id=1, source_target_pairs={{0,17},{1,16},{2,19},{3,18},{4,21},{5,20},{6,23},{7,22},{8,25},{9,... | collective-permute-start | bytes 1769480 | tf_op jit(solution)/shard_map/ppermute | solution.py:33
  80.6 82.7 %collective-permute-start.31 = (bf16[288,1024]{1,0:T(8,128)(2,1)S(1)}, bf16[288,1024]{1,0:T(8,128)(2,1)S(1)}, u32[]{:S(2)}, u32[]{:S(2)}) collective-permute-start(bf16[288,1024]{1,0:T(8,128)(2,1)S(1)} %get-tuple-element.81), channel_id=1, source_target_pairs={{0,1},{1,0},{2,3},{3,2},{4,5},{5,4},{6,7},{7,6},{8,9},{9,8},{10,11... | collective-permute-start | bytes 1769480 | tf_op jit(solution)/shard_map/ppermute | solution.py:33
  93.5 70.8 %collective-permute-start.32 = (bf16[288,1024]{1,0:T(8,128)(2,1)S(1)}, bf16[288,1024]{1,0:T(8,128)(2,1)S(1)}, u32[]{:S(2)}, u32[]{:S(2)}) collective-permute-start(bf16[288,1024]{1,0:T(8,128)(2,1)S(1)} %get-tuple-element.82), channel_id=1, source_target_pairs={{0,2},{1,3},{2,0},{3,1},{4,6},{5,7},{6,4},{7,5},{8,10},{9,11},{10,... | collective-permute-start | bytes 1769480 | tf_op jit(solution)/shard_map/ppermute | solution.py:33
  95.0 76.3 %collective-permute-start.33 = (bf16[288,1024]{1,0:T(8,128)(2,1)S(1)}, bf16[288,1024]{1,0:T(8,128)(2,1)S(1)}, u32[]{:S(2)}, u32[]{:S(2)}) collective-permute-start(bf16[288,1024]{1,0:T(8,128)(2,1)S(1)} %get-tuple-element.83), channel_id=1, source_target_pairs={{0,3},{1,2},{2,1},{3,0},{4,7},{5,6},{6,5},{7,4},{8,11},{9,10},{10,... | collective-permute-start | bytes 1769480 | tf_op jit(solution)/shard_map/ppermute | solution.py:33
  95.2 82.6 %collective-permute-start.37 = (bf16[288,1024]{1,0:T(8,128)(2,1)S(1)}, bf16[288,1024]{1,0:T(8,128)(2,1)S(1)}, u32[]{:S(2)}, u32[]{:S(2)}) collective-permute-start(bf16[288,1024]{1,0:T(8,128)(2,1)S(1)} %get-tuple-element.87), channel_id=1, source_target_pairs={{0,1},{1,0},{2,3},{3,2},{4,5},{5,4},{6,7},{7,6},{8,9},{9,8},{10,11... | collective-permute-start | bytes 1769480 | tf_op jit(solution)/shard_map/ppermute | solution.py:33
  177.8 35.2 %collective-permute-start.43 = (bf16[288,1024]{1,0:T(8,128)(2,1)}, bf16[288,1024]{1,0:T(8,128)(2,1)}, u32[]{:S(2)}, u32[]{:S(2)}) collective-permute-start(bf16[288,1024]{1,0:T(8,128)(2,1)} %get-tuple-element.93), channel_id=1, source_target_pairs={{0,1},{1,0},{2,3},{3,2},{4,5},{5,4},{6,7},{7,6},{8,9},{9,8},{10,11... | collective-permute-start | bytes 1769480 | tf_op jit(solution)/shard_map/ppermute | solution.py:33
  181.5 73.4 %collective-permute-start.16 = (bf16[512,1024]{1,0:T(8,128)(2,1)}, bf16[512,1024]{1,0:T(8,128)(2,1)}, u32[]{:S(2)}, u32[]{:S(2)}) collective-permute-start(bf16[512,1024]{1,0:T(8,128)(2,1)} %partial_sums.20), channel_id=1, source_target_pairs={{0,2},{1,3},{2,0},{3,1},{4,6},{5,7},{6,4},{7,5},{8,10},{9,11},{10,... | collective-permute-start | bytes 3145736 | tf_op jit(solution)/shard_map/ppermute | solution.py:33
  192.7 37.2 %collective-permute-start.44 = (bf16[288,1024]{1,0:T(8,128)(2,1)}, bf16[288,1024]{1,0:T(8,128)(2,1)S(1)}, u32[]{:S(2)}, u32[]{:S(2)}) collective-permute-start(bf16[288,1024]{1,0:T(8,128)(2,1)} %copy-done.54), channel_id=1, source_target_pairs={{0,2},{1,3},{2,0},{3,1},{4,6},{5,7},{6,4},{7,5},{8,10},{9,11},{10,... | collective-permute-start | bytes 1769480 | tf_op jit(solution)/shard_map/ppermute | solution.py:33
  202.8 40.4 %collective-permute-start.45 = (bf16[288,1024]{1,0:T(8,128)(2,1)}, bf16[288,1024]{1,0:T(8,128)(2,1)S(1)}, u32[]{:S(2)}, u32[]{:S(2)}) collective-permute-start(bf16[288,1024]{1,0:T(8,128)(2,1)} %copy-done.53), channel_id=1, source_target_pairs={{0,3},{1,2},{2,1},{3,0},{4,7},{5,6},{6,5},{7,4},{8,11},{9,10},{10,... | collective-permute-start | bytes 1769480 | tf_op jit(solution)/shard_map/ppermute | solution.py:33
  216.5 42.7 %collective-permute-start.22 = (bf16[512,1024]{1,0:T(8,128)(2,1)}, bf16[512,1024]{1,0:T(8,128)(2,1)}, u32[]{:S(2)}, u32[]{:S(2)}) collective-permute-start(bf16[512,1024]{1,0:T(8,128)(2,1)} %partial_sums.22), channel_id=1, source_target_pairs={{0,16},{1,17},{2,18},{3,19},{4,20},{5,21},{6,22},{7,23},{8,24},{9,... | collective-permute-start | bytes 3145736 | tf_op jit(solution)/shard_map/ppermute | solution.py:33
  221.2 43.9 %collective-permute-start.28 = (bf16[512,1024]{1,0:T(8,128)(2,1)}, bf16[512,1024]{1,0:T(8,128)(2,1)}, u32[]{:S(2)}, u32[]{:S(2)}) collective-permute-start(bf16[512,1024]{1,0:T(8,128)(2,1)} %partial_sums.24), channel_id=1, source_target_pairs={{0,2},{1,3},{2,0},{3,1},{4,6},{5,7},{6,4},{7,5},{8,10},{9,11},{10,... | collective-permute-start | bytes 3145736 | tf_op jit(solution)/shard_map/ppermute | solution.py:33
  253.4 34.1 %collective-permute-start.40 = (bf16[512,1024]{1,0:T(8,128)(2,1)}, bf16[512,1024]{1,0:T(8,128)(2,1)}, u32[]{:S(2)}, u32[]{:S(2)}) collective-permute-start(bf16[512,1024]{1,0:T(8,128)(2,1)} %partial_sums.28), channel_id=1, source_target_pairs={{0,2},{1,3},{2,0},{3,1},{4,6},{5,7},{6,4},{7,5},{8,10},{9,11},{10,... | collective-permute-start | bytes 3145736 | tf_op jit(solution)/shard_map/ppermute | solution.py:33
  254.9 44.7 %collective-permute-start.46 = (bf16[512,1024]{1,0:T(8,128)(2,1)}, bf16[512,1024]{1,0:T(8,128)(2,1)}, u32[]{:S(2)}, u32[]{:S(2)}) collective-permute-start(bf16[512,1024]{1,0:T(8,128)(2,1)} %partial_sums.30), channel_id=1, source_target_pairs={{0,16},{1,17},{2,18},{3,19},{4,20},{5,21},{6,22},{7,23},{8,24},{9,... | collective-permute-start | bytes 3145736 | tf_op jit(solution)/shard_map/ppermute | solution.py:33
  259.2 43.6 %collective-permute-start.17 = (bf16[256,1024]{1,0:T(8,128)(2,1)S(1)}, bf16[256,1024]{1,0:T(8,128)(2,1)S(1)}, u32[]{:S(2)}, u32[]{:S(2)}) collective-permute-start(bf16[256,1024]{1,0:T(8,128)(2,1)S(1)} %get-tuple-element.67), channel_id=1, source_target_pairs={{0,4},{1,5},{2,6},{3,7},{4,0},{5,1},{6,2},{7,3},{8,12},{9,13},{10,... | collective-permute-start | bytes 1572872 | tf_op jit(solution)/shard_map/ppermute | solution.py:33
  265.1 39.4 %collective-permute-start.23 = (bf16[256,1024]{1,0:T(8,128)(2,1)S(1)}, bf16[256,1024]{1,0:T(8,128)(2,1)S(1)}, u32[]{:S(2)}, u32[]{:S(2)}) collective-permute-start(bf16[256,1024]{1,0:T(8,128)(2,1)S(1)} %get-tuple-element.73), channel_id=1, source_target_pairs={{0,4},{1,5},{2,6},{3,7},{4,0},{5,1},{6,2},{7,3},{8,12},{9,13},{10,... | collective-permute-start | bytes 1572872 | tf_op jit(solution)/shard_map/ppermute | solution.py:33
  299.6 34.6 %collective-permute-start.41 = (bf16[256,1024]{1,0:T(8,128)(2,1)S(1)}, bf16[256,1024]{1,0:T(8,128)(2,1)S(1)}, u32[]{:S(2)}, u32[]{:S(2)}) collective-permute-start(bf16[256,1024]{1,0:T(8,128)(2,1)S(1)} %get-tuple-element.91), channel_id=1, source_target_pairs={{0,4},{1,5},{2,6},{3,7},{4,0},{5,1},{6,2},{7,3},{8,12},{9,13},{10,... | collective-permute-start | bytes 1572872 | tf_op jit(solution)/shard_map/ppermute | solution.py:33
  302.8 42.8 %collective-permute-start.47 = (bf16[256,1024]{1,0:T(8,128)(2,1)S(1)}, bf16[256,1024]{1,0:T(8,128)(2,1)S(1)}, u32[]{:S(2)}, u32[]{:S(2)}) collective-permute-start(bf16[256,1024]{1,0:T(8,128)(2,1)S(1)} %get-tuple-element.97), channel_id=1, source_target_pairs={{0,4},{1,5},{2,6},{3,7},{4,0},{5,1},{6,2},{7,3},{8,12},{9,13},{10,... | collective-permute-start | bytes 1572872 | tf_op jit(solution)/shard_map/ppermute | solution.py:33
  304.6 41.4 %collective-permute-start.18 = (bf16[128,1024]{1,0:T(8,128)(2,1)S(1)}, bf16[128,1024]{1,0:T(8,128)(2,1)S(1)}, u32[]{:S(2)}, u32[]{:S(2)}) collective-permute-start(bf16[128,1024]{1,0:T(8,128)(2,1)S(1)} %slice.85), channel_id=1, source_target_pairs={{0,8},{1,9},{2,10},{3,11},{4,12},{5,13},{6,14},{7,15},{8,0},{9,1},... | collective-permute-start | bytes 786440 | tf_op jit(solution)/shard_map/ppermute | solution.py:33
  306.9 42.1 %collective-permute-start.24 = (bf16[128,1024]{1,0:T(8,128)(2,1)S(1)}, bf16[128,1024]{1,0:T(8,128)(2,1)S(1)}, u32[]{:S(2)}, u32[]{:S(2)}) collective-permute-start(bf16[128,1024]{1,0:T(8,128)(2,1)S(1)} %slice.87), channel_id=1, source_target_pairs={{0,8},{1,9},{2,10},{3,11},{4,12},{5,13},{6,14},{7,15},{8,0},{9,1},... | collective-permute-start | bytes 786440 | tf_op jit(solution)/shard_map/ppermute | solution.py:33
  307.5 42.3 %collective-permute-start.30 = (bf16[128,1024]{1,0:T(8,128)(2,1)S(1)}, bf16[128,1024]{1,0:T(8,128)(2,1)S(1)}, u32[]{:S(2)}, u32[]{:S(2)}) collective-permute-start(bf16[128,1024]{1,0:T(8,128)(2,1)S(1)} %slice.89), channel_id=1, source_target_pairs={{0,8},{1,9},{2,10},{3,11},{4,12},{5,13},{6,14},{7,15},{8,0},{9,1},... | collective-permute-start | bytes 786440 | tf_op jit(solution)/shard_map/ppermute | solution.py:33
  334.2 36.4 %collective-permute-start.36 = (bf16[128,1024]{1,0:T(8,128)(2,1)S(1)}, bf16[128,1024]{1,0:T(8,128)(2,1)S(1)}, u32[]{:S(2)}, u32[]{:S(2)}) collective-permute-start(bf16[128,1024]{1,0:T(8,128)(2,1)S(1)} %slice.91), channel_id=1, source_target_pairs={{0,8},{1,9},{2,10},{3,11},{4,12},{5,13},{6,14},{7,15},{8,0},{9,1},... | collective-permute-start | bytes 786440 | tf_op jit(solution)/shard_map/ppermute | solution.py:33
  346.0 35.9 %collective-permute-start.48 = (bf16[128,1024]{1,0:T(8,128)(2,1)S(1)}, bf16[128,1024]{1,0:T(8,128)(2,1)S(1)}, u32[]{:S(2)}, u32[]{:S(2)}) collective-permute-start(bf16[128,1024]{1,0:T(8,128)(2,1)S(1)} %slice.95), channel_id=1, source_target_pairs={{0,8},{1,9},{2,10},{3,11},{4,12},{5,13},{6,14},{7,15},{8,0},{9,1},... | collective-permute-start | bytes 786440 | tf_op jit(solution)/shard_map/ppermute | solution.py:33
  (92 other events, 1155.7 us)
Sparse Core Ops, SparseCore 0:
  186.8 32.0 all-gather.2

commit v2 on v0

v2 whole, which is shorter than its diff:
```python
import functools
import math

import jax
import jax.numpy as jnp
from jax import lax
from jax.experimental import pallas as pl
from jax.experimental.pallas import tpu as pltpu
from jax.sharding import PartitionSpec as P

LATENT_WIDTH = 512
PLAIN_HEAD_WIDTH = 128
ROTARY_WIDTH = 64
VALUE_WIDTH = 128
EXP_DEV = 3
ROUTE_SCALE = 2.827
AXES = ("ctx", "exp")
VMEM_LIMIT = 60 * 1024 * 1024
SMALL = pl.CostEstimate(flops=0, bytes_accessed=0, transcendentals=0)
LARGE = pl.CostEstimate(flops=10**12, bytes_accessed=0, transcendentals=0)

STEPS = ((768, True), (1536, True), (1792, True), (1536, True), (1024, False), (512, False))
QUERY_BLOCKS = (0, 3, 3, 2, 0, 0)
LONG_PACKS = (1, 2)
SENDS = (4, 2, 5, 3, 1, 6, 7)
IN_FLIGHT = 5


def after(value, *others):
    return lax.optimization_barrier((value, *others))[0]


def exchange(value, mask, devices):
    return lax.ppermute(value, AXES, [(i, i ^ mask) for i in range(devices)])


def tile_of(start, width):
    for tile in (512, 256, 128):
        if start % tile == 0 and width % tile == 0:
            return tile
    raise ValueError("columns")


def pack_kernel(ctx_ref, select_ref, near_ref, far_ref, *outs):
    for far, ref in enumerate((near_ref, far_ref)):
        rows = jnp.dot(select_ref[...], ref[0], preferred_element_type=jnp.float32)
        lines = rows.shape[0] // 4
        for q in range(4):
            outs[4 * far + q][...] = rows[q * lines : (q + 1) * lines].astype(jnp.bfloat16)


def pack(ctx, select, rows, start, width, long):
    depth = rows.shape[1]
    tile = tile_of(start, width)
    block = start // tile
    return pl.pallas_call(
        pack_kernel,
        grid_spec=pltpu.PrefetchScalarGridSpec(
            num_scalar_prefetch=1,
            grid=(width // tile,),
            in_specs=[
                pl.BlockSpec((depth, depth), lambda j, ctx: (0, 0)),
                pl.BlockSpec((1, depth, tile), lambda j, ctx: (ctx[0], 0, block + j)),
                pl.BlockSpec((1, depth, tile), lambda j, ctx: (1 - ctx[0], 0, block + j)),
            ],
            out_specs=[pl.BlockSpec((depth // 4, tile), lambda j, ctx: (0, j))] * 8,
        ),
        out_shape=[jax.ShapeDtypeStruct((depth // 4, width), rows.dtype)] * 8,
        compiler_params=pltpu.CompilerParams(vmem_limit_bytes=VMEM_LIMIT),
        cost_estimate=LARGE if long else SMALL,
        name="pack_rows",
    )(ctx, select, rows, rows)


def weights_kernel(count, capacity, across, me_ref, routes_ref, out_ref):
    tokens = routes_ref.shape[2]
    topk = routes_ref.shape[1] // 2
    ids = routes_ref[0, :topk, :]
    gates = routes_ref[0, topk:, :]
    scaled = ROUTE_SCALE * gates / jnp.sum(gates, axis=0, keepdims=True)
    before = lax.broadcasted_iota(jnp.int32, (tokens, tokens), 0) < lax.broadcasted_iota(
        jnp.int32, (tokens, tokens), 1
    )
    before = jnp.where(before, 1.0, 0.0).astype(jnp.bfloat16)
    row = lax.broadcasted_iota(jnp.int32, (count * capacity, tokens), 0)
    row = (row - pl.program_id(0) * capacity).astype(jnp.float32)
    totals = []
    for source in range(8):
        owner = me_ref[0] ^ ((source & 3) | (across if source & 4 else 0))
        low = (owner * EXP_DEV).astype(jnp.float32)
        match = jnp.where((ids >= low) & (ids < low + EXP_DEV), 1.0, 0.0)
        per_token = jnp.broadcast_to(jnp.sum(match, axis=0, keepdims=True), match.shape)
        prior = jnp.dot(
            per_token.astype(jnp.bfloat16), before, preferred_element_type=jnp.float32
        )
        slot = prior[0:1, :]
        total = jnp.zeros((count * capacity, tokens), jnp.float32)
        for k in range(topk):
            weight = scaled[k : k + 1, :] * match[k : k + 1, :]
            total = total + jnp.where(row == slot, weight, 0.0)
            slot = slot + match[k : k + 1, :]
        totals.append(total)
    out_ref[...] = jnp.concatenate(totals, axis=0).T.astype(jnp.bfloat16)


def combine_weights(me, routes, capacity, across):
    count, lines, tokens = routes.shape

    def place(i, me_ref):
        return (i ^ ((me_ref[0] >> 2) & (count - 1)), 0, 0)

    return pl.pallas_call(
        functools.partial(weights_kernel, count, capacity, across),
        grid_spec=pltpu.PrefetchScalarGridSpec(
            num_scalar_prefetch=1,
            grid=(count,),
            in_specs=[pl.BlockSpec((1, lines, tokens), place)],
            out_specs=pl.BlockSpec((tokens, 8 * count * capacity), lambda i, me_ref: (i, 0)),
        ),
        out_shape=jax.ShapeDtypeStruct((count * tokens, 8 * count * capacity), jnp.bfloat16),
        compiler_params=pltpu.CompilerParams(vmem_limit_bytes=VMEM_LIMIT),
        cost_estimate=SMALL,
        name="combine_weights",
    )(me, routes)


def sums_kernel(tokens, side_ref, weights_ref, *refs):
    rows = jnp.concatenate([ref[...] for ref in refs[:8]], axis=0)
    total = jnp.dot(weights_ref[...], rows, preferred_element_type=jnp.float32)
    outs = refs[8:]
    if len(outs) == 1:
        outs[0][...] = total.astype(outs[0].dtype)
        return
    first = side_ref[0] == 0
    for pair in range(total.shape[0] // (2 * tokens)):
        even = total[2 * pair * tokens : (2 * pair + 1) * tokens]
        odd = total[(2 * pair + 1) * tokens : (2 * pair + 2) * tokens]
        here = slice(pair * tokens, (pair + 1) * tokens)
        outs[0][here, :] = jnp.where(first, even, odd).astype(outs[0].dtype)
        outs[1][here, :] = jnp.where(first, odd, even).astype(outs[1].dtype)


def partial_sums(weights, rows, side, tokens, split):
    out_rows, depth = weights.shape
    width = rows[0].shape[1]
    tile = tile_of(0, width)
    parts = 2 if split else 1
    return pl.pallas_call(
        functools.partial(sums_kernel, tokens),
        grid_spec=pltpu.PrefetchScalarGridSpec(
            num_scalar_prefetch=1,
            grid=(width // tile,),
            in_specs=[pl.BlockSpec((out_rows, depth), lambda j, side: (0, 0))]
            + [pl.BlockSpec((depth // 8, tile), lambda j, side: (0, j))] * 8,
            out_specs=[pl.BlockSpec((out_rows // parts, tile), lambda j, side: (0, j))] * parts,
        ),
        out_shape=[jax.ShapeDtypeStruct((out_rows // parts, width), jnp.bfloat16)] * parts,
        compiler_params=pltpu.CompilerParams(vmem_limit_bytes=VMEM_LIMIT),
        cost_estimate=SMALL,
        name="partial_sums",
    )(side, weights, *rows)


def attention_kernel(
    scale, first, info, queries_ref, key_up_ref, value_up_ref, own_ref, other_ref, out_ref,
    keys_ref, full_ref, scores_ref, lane_ref, weight_ref, sems,
):
    blocks = sems.shape[0]
    block_len = queries_ref.shape[0]
    step = pl.program_id(0)
    tile = scores_ref.shape[2]
    lanes = lane_ref.shape[1]

    def copy_of(p, source):
        begin = pl.multiple_of(info[1 + blocks + p] * block_len, block_len)
        return pltpu.make_async_copy(
            source.at[pl.ds(begin, block_len)],
            keys_ref.at[pl.ds(pl.multiple_of(p * block_len, block_len), block_len)],
            sems.at[p],
        )

    @pl.when(step == 0)
    def _():
        for p in range(blocks):
            pl.when(info[1 + p] == info[0])(lambda: copy_of(p, own_ref).start())
            pl.when(info[1 + p] != info[0])(lambda: copy_of(p, other_ref).start())

    queries = queries_ref[...]
    full_ref[:, :LATENT_WIDTH] = jnp.dot(
        queries[:, :PLAIN_HEAD_WIDTH], key_up_ref[...], preferred_element_type=jnp.float32
    ).astype(jnp.bfloat16)
    full_ref[:, LATENT_WIDTH:] = queries[:, PLAIN_HEAD_WIDTH:]

    place = info[1 + 2 * blocks + first + step]
    last = place * block_len // tile

    def wait_for(t):
        @pl.when(step == 0)
        def _():
            for p in range(tile // block_len):
                copy_of(t * (tile // block_len) + p, own_ref).wait()
    factor = scale * math.log2(math.e)

    def keys_of(t):
        return keys_ref[pl.ds(pl.multiple_of(t * tile, tile), tile), :]

    def lane_parts(values):
        return [values[:, i * lanes : (i + 1) * lanes] for i in range(tile // lanes)]

    def score(t, masked):
        scores = lax.dot_general(
            full_ref[...], keys_of(t), (((1,), (1,)), ((), ())), preferred_element_type=jnp.float32
        )
        if masked:
            key = lax.broadcasted_iota(jnp.int32, scores.shape, 1) + t * tile
            query = lax.broadcasted_iota(jnp.int32, scores.shape, 0) + place * block_len
            scores = jnp.where(key <= query, scores, -1e30)
        scores_ref[t] = scores
        lane_ref[...] = functools.reduce(jnp.maximum, lane_parts(scores), lane_ref[...])

    lane_ref[...] = jnp.full(lane_ref.shape, -1e30, jnp.float32)

    @pl.loop(0, last)
    def _(t):
        wait_for(t)
        score(t, False)

    wait_for(last)
    score(last, True)
    highest = jnp.max(lane_ref[...], axis=1, keepdims=True) * factor
    lane_ref[...] = jnp.zeros(lane_ref.shape, jnp.float32)
    weight_ref[...] = jnp.zeros(weight_ref.shape, jnp.float32)

    @pl.loop(0, last + 1)
    def _(t):
        probs = jnp.exp2(scores_ref[t] * factor - highest)
        lane_ref[...] = functools.reduce(jnp.add, lane_parts(probs), lane_ref[...])
        weight_ref[...] += jnp.dot(
            probs.astype(jnp.bfloat16),
            keys_of(t)[:, :LATENT_WIDTH],
            preferred_element_type=jnp.float32,
        )

    weight_sum = jnp.sum(lane_ref[...], axis=1, keepdims=True)
    latent_out = (weight_ref[...] / weight_sum).astype(jnp.bfloat16)
    out_ref[...] = jnp.dot(
        latent_out, value_up_ref[...], preferred_element_type=jnp.float32
    ).astype(out_ref.dtype)

    @pl.loop(last + 1, scores_ref.shape[0])
    def _(t):
        wait_for(t)


def attend(queries, own, other, key_up, value_up, info, blocks, first, count):
    block_len = 2 * own.shape[0] // blocks
    head_width = queries.shape[1]
    tile = 2 * block_len
    hbm = pl.BlockSpec(memory_space=pl.ANY)
    return pl.pallas_call(
        functools.partial(
            attention_kernel, 1.0 / math.sqrt(PLAIN_HEAD_WIDTH + ROTARY_WIDTH), first
        ),
        grid_spec=pltpu.PrefetchScalarGridSpec(
            num_scalar_prefetch=1,
            grid=(count,),
            in_specs=[
                pl.BlockSpec((block_len, head_width), lambda i, info: (first + i, 0)),
                pl.BlockSpec(key_up.shape, lambda i, info: (0, 0)),
                pl.BlockSpec(value_up.shape, lambda i, info: (0, 0)),
                hbm,
                hbm,
            ],
            out_specs=pl.BlockSpec((block_len, VALUE_WIDTH), lambda i, info: (i, 0)),
            scratch_shapes=[
                pltpu.VMEM((blocks * block_len, own.shape[1]), jnp.bfloat16),
                pltpu.VMEM((block_len, own.shape[1]), jnp.bfloat16),
                pltpu.VMEM((blocks * block_len // tile, block_len, tile), jnp.float32),
                pltpu.VMEM((block_len, 128), jnp.float32),
                pltpu.VMEM((block_len, LATENT_WIDTH), jnp.float32),
                pltpu.SemaphoreType.DMA((blocks,)),
            ],
        ),
        out_shape=jax.ShapeDtypeStruct((count * block_len, VALUE_WIDTH), jnp.bfloat16),
        compiler_params=pltpu.CompilerParams(vmem_limit_bytes=VMEM_LIMIT),
        cost_estimate=LARGE,
        name="latent_attention",
    )(info, queries, key_up, value_up, own, other)


def shards(
    queries, latent, key_up_weight, value_up_weight, block_order, expert_ids, gates, expert_rows
):
    n_ctx, n_exp = lax.axis_size("ctx"), lax.axis_size("exp")
    devices = n_ctx * n_exp
    ctx = lax.axis_index("ctx").astype(jnp.int32)
    exp = lax.axis_index("exp").astype(jnp.int32)
    me = (ctx * n_exp + exp).reshape(1)
    capacity, model_width = expert_rows.shape[4:]
    rows = jnp.transpose(expert_rows[0, 0], (0, 2, 1, 3)).reshape(n_ctx, capacity * n_exp, model_width)
    count = n_exp // 4
    slots = jnp.arange(n_exp * capacity, dtype=jnp.int32)
    relative = slots // (count * capacity)
    low_bits = (exp & 3) ^ relative
    wanted = (slots % capacity) * n_exp + (slots // capacity) % count * 4 + low_bits
    select = (wanted[:, None] == slots[None, :]).astype(jnp.bfloat16)

    ctx1, side = ctx.reshape(1), ((exp >> 2) & 1).reshape(1)
    steps, tokens = len(STEPS), expert_ids.shape[0]
    packed, held, sent = [None] * steps, [[None] * 8 for _ in STEPS], []

    def pack_step(i, *others):
        start = sum(width for width, _ in STEPS[:i])
        return pack(after(ctx1, *others), select, rows, start, STEPS[i][0], i in LONG_PACKS)

    def send(i, parts, *others):
        for part in parts:
            mask = (part & 3) | (n_exp if part & 4 else 0)
            queue = sent[-IN_FLIGHT : 1 - IN_FLIGHT]
            held[i][part] = exchange(after(packed[i][part], *queue, *others), mask, devices)
            sent.append(held[i][part])

    packed[0] = pack_step(0)

    routes = jnp.concatenate([expert_ids.T.astype(jnp.float32), gates.T], axis=0)[None]
    routes = after(routes, packed[0][0])
    for bit in range(2, n_exp.bit_length() - 1):
        routes = jnp.concatenate([routes, exchange(routes, 1 << bit, devices)], axis=0)
    send(0, SENDS[:4])
    packed[1] = pack_step(1, packed[0][0])
    weights = combine_weights(after(me, packed[1][0]), routes, capacity, n_exp)
    send(0, SENDS[4:])
    send(1, SENDS[:4])
    last = [weights]

    latent = after(latent, packed[1][0])
    members = n_exp // 2
    share = latent.shape[0] // members
    place = (exp >> 2) * 2 + (exp & 1)
    mine = lax.dynamic_slice_in_dim(latent, place * share, share, axis=0)
    part = exchange(after(mine, *sent[:2]), n_exp, devices)
    groups = [[d for d in range(n_exp) if (d >> 1) & 1 == bit] for bit in range(2)]
    other = lax.all_gather(
        after(part, *sent[4:7]), "exp", axis=0, tiled=True, axis_index_groups=groups
    )

    blocks = block_order.shape[0]
    local_blocks = blocks // n_ctx
    ids = jnp.arange(blocks, dtype=jnp.int32)
    stored = jnp.sum(jnp.where(block_order[None, :] == ids[:, None], ids[None, :], 0), axis=1)
    query_block = lax.dynamic_slice_in_dim(block_order, ctx * local_blocks, local_blocks)
    info = jnp.concatenate([ctx1, stored // local_blocks, stored % local_blocks, query_block])
    heads = key_up_weight.shape[0]
    head_width = PLAIN_HEAD_WIDTH + ROTARY_WIDTH
    outputs, done_blocks = [], 0

    def attention_part(count, *last):
        nonlocal done_blocks
        part = []
        for h in range(heads):
            head_queries = queries[:, h * head_width : (h + 1) * head_width]
            part.append(
                attend(
                    head_queries,
                    latent,
                    other,
                    key_up_weight[h],
                    value_up_weight[h],
                    after(info, *last),
                    blocks,
                    done_blocks,
                    count,
                )
            )
        done_blocks += count
        outputs.append(part[0] if heads == 1 else jnp.concatenate(part, axis=1))
        return outputs[-1]

    def halve(total, bit):
        place = (exp >> bit) & 1
        pairs = total.reshape(-1, 2, tokens, total.shape[1])
        halves = (lax.dynamic_index_in_dim(pairs, p, 1, keepdims=False) for p in (place, 1 - place))
        return [half.reshape(-1, total.shape[1]) for half in halves]

    bits = range(2, n_exp.bit_length() - 1)
    halves = [None] * steps
    pieces = [None] * steps

    def begin(i, keep, send, bit, *others):
        halves[i] = (keep, exchange(after(send, *others), 1 << bit, devices), bit)

    def advance(i, *others):
        keep, got, bit = halves[i]
        keep = after(keep, *others)
        total = (keep.astype(jnp.float32) + got.astype(jnp.float32)).astype(jnp.bfloat16)
        if bit == bits[-1]:
            pieces[i] = total
        else:
            begin(i, *halve(total, bit + 1), bit + 1)

    axis_groups = [list(range(low, n_exp, 4)) for low in range(4)]
    for i, (_, scattered) in enumerate(STEPS):
        held[i][0] = packed[i][0]
        ready = [part] if i == 0 else []
        sums = partial_sums(weights, held[i], after(side, *last, *ready), tokens, not scattered)
        last = sums[:1]
        if i + 1 < steps:
            send(i + 1, SENDS[4:], *last)
        if QUERY_BLOCKS[i]:
            last = [attention_part(QUERY_BLOCKS[i], *last, pieces[i - 1])]
        if i + 2 < steps:
            packed[i + 2] = pack_step(i + 2, *last)
            last = packed[i + 2][:1]
            send(i + 2, SENDS[:4])
        if not scattered:
            begin(i, *sums, bits[0])
        else:
            pieces[i] = lax.psum_scatter(
                after(sums[0], held[i + 1][SENDS[0]], held[i + 1][SENDS[1]]),
                "exp",
                scatter_dimension=0,
                axis_index_groups=axis_groups,
                tiled=True,
            )
    pieces = [piece if piece is None else after(piece, *last) for piece in pieces]
    while any(piece is None for piece in pieces):
        before = ()
        for i in range(steps):
            if pieces[i] is None:
                advance(i, *before)
                before = (halves[i][0] if pieces[i] is None else pieces[i],)
    combined = jnp.concatenate(pieces, axis=1)
    attended = jnp.concatenate(outputs, axis=0)
    return (attended, combined)


def solution(mesh):
    return jax.shard_map(
        shards,
        mesh=mesh,
        in_specs=(
            P("ctx", "exp"),
            P("ctx", None),
            P("exp", None, None),
            P("exp", None, None),
            P(),
            P(("ctx", "exp"), None),
            P(("ctx", "exp"), None),
            P("ctx", "exp", None, None, None, None),
        ),
        out_specs=(P("ctx", "exp"), P(("ctx", "exp"), None)),
        check_vma=False,
    )
```

time: 599 us -> 283 us (0.47); the launches traced: 588 us -> 279 us
  waiting for transfers between devices: 328 us -> 77.8 us
  local copies, waits for them, and re-layouts: 161 us -> 8.14 us
  Pallas kernels: 0 us -> 107 us
  starting transfers between devices: 6.53 us -> 66.9 us
  matrix products: 43.4 us -> 0 us
  other arithmetic: 34.7 us -> 3.64 us
    all_gather x1, waiting for transfers between devices: 197 us -> 0.02 us  [shards(): lax.all_gather(after(part, *sent[4:7]), 'exp', axis=0, tiled=True, axis_i...]
    all_to_all x1 -> x0, waiting for transfers between devices: 130 us -> none  [shards(): lax.all_to_all(expert_rows.reshape(devices, capacity, model_width), ('ctx...]
    gather x8 -> x0, local copies, waits for them, and re-layouts: 108 us -> none  [shards(): picked = jnp.take(returned, owners[:, k] * capacity + slots[:, k], axis=0)]
    pallas_call x0 -> x16, Pallas kernels: none -> 107 us  [the longest x3 35.7 us: attend(): pl.pallas_call(functools.partial(attention_kernel, 1.0 / math.sqrt(PLAIN_...]
    ppermute x0 -> x49, waiting for transfers between devices: none -> 77.6 us  [exchange(): return lax.ppermute(value, AXES, [(i, i ^ mask) for i in range(devices)])]
    ppermute x0 -> x49, starting transfers between devices: none -> 66.5 us  [exchange(): return lax.ppermute(value, AXES, [(i, i ^ mask) for i in range(devices)])]
    reshape x3 -> x2, local copies, waits for them, and re-layouts: 44 us -> 0.07 us  [halve(): return [half.reshape(-1, total.shape[1]) for half in halves]]
    dot_general x3 -> x0, matrix products: 43.4 us -> none  [the longest x1 23 us: shards(): jnp.einsum('thc,sc->hts', query_full, key_segment, preferred_element_type...]
  transfers between devices with their start and end apart: 2 -> 54, of which waited for: 2 -> 15; matrix products, arithmetic and copies ran while one was open for 12% -> 3% of each run, Pallas kernels for 0% -> 37%
where the time goes in v2:
time: 283 us; the launch traced here: 279 us
  Pallas kernels  107 us (38%)
  waiting for transfers between devices  77.8 us (27%)
  starting transfers between devices  66.9 us (24%)
  between operations  15.8 us (6%)
  local copies, waits for them, and re-layouts  8.14 us (3%)
  other arithmetic  3.64 us (1%)
    ppermute x49, waiting for transfers between devices, exchange(): return lax.ppermute(value, AXES, [(i, i ^ mask) for i in range(devices)])  77.6 us
    ppermute x49, starting transfers between devices, exchange(): return lax.ppermute(value, AXES, [(i, i ^ mask) for i in range(devices)])  66.5 us
    pallas_call x3, Pallas kernels, attend(): pl.pallas_call(functools.partial(attention_kernel, 1.0 / math.sqrt(PLAIN_...  35.7 us
    pallas_call x6, Pallas kernels, pack(): pl.pallas_call(pack_kernel, grid_spec=pltpu.PrefetchScalarGridSpec(num_sc...  34 us
    pallas_call x6, Pallas kernels, partial_sums(): pl.pallas_call(functools.partial(sums_kernel, tokens), grid_spec=pltpu.Pr...  32.9 us
  transfers between devices with their start and end apart: 54, of which 15 were waited for; matrix products, arithmetic and copies ran while one was open for 3% of the time, Pallas kernels for 37%

profile of v2, /device:TPU:3, one launch (start us, length us, event | category | flops | bytes accessed | tf_op | source)
XLA Modules:
  0.0 279.1 jit_solution(3325917599602309642)
XLA Ops:
  9.2 4.5 %pack_rows.6 = (bf16[144,768]{1,0:T(8,128)(2,1)}, bf16[144,768]{1,0:T(8,128)(2,1)}, bf16[144,768]{1,0:T(8,128)(2,1)}, bf16[144,768]{1,0:T(8,128)(2,1)}, bf16[144...) custom-call(s32[1]{0:T(128)} %bitcast.ctx_ref, ...), custom_call_target="tpu_custom_call" | custom-call | tf_op jit(solution)/shard_map/pack_rows/pallas_call | solution.py:56
  17.6 7.1 %pack_rows.7 = (bf16[144,1536]{1,0:T(8,128)(2,1)}, bf16[144,1536]{1,0:T(8,128)(2,1)}, bf16[144,1536]{1,0:T(8,128)(2,1)}, bf16[144,1536]{1,0:T(8,128)(2,1)}, bf16...) custom-call(s32[1]{0:T(128)} %bitcast.ctx_ref, ...), custom_call_target="tpu_custom_call" | custom-call | flops 999999995904 | tf_op jit(solution)/shard_map/pack_rows/pallas_call | solution.py:56
  43.3 4.3 %combine_weights.1.weights_ref = bf16[512,1152]{1,0:T(8,128)(2,1)} custom-call(s32[1]{0:T(128)} %bitcast.2.me_ref, f32[4,16,128]{2,1,0:T(8,128)} %pad_maximum_fusion.1.routes_ref), custom_call_target="tpu_custom_call" | custom-call | tf_op jit(solution)/shard_map/combine_weights/pallas_call | solution.py:112
  47.6 6.2 %collective-permute-done.9.refs_7_ = bf16[144,768]{1,0:T(8,128)(2,1)} collective-permute-done((bf16[144,768]{1,0:T(8,128)(2,1)}, bf16[144,768]{1,0:T(8,128)(2,1)}, u32[]{:S(2)}, u32[]{:S(2)}) %collective-permute-start.9) | collective-permute-done | bytes 221216 | tf_op jit(solution)/shard_map/ppermute | solution.py:34
  55.3 4.7 %partial_sums.6 = bf16[512,768]{1,0:T(8,128)(2,1)} custom-call(s32[1]{0:T(128)} %bitcast.1.side_ref, bf16[512,1152]{1,0:T(8,128)(2,1)} %combine_weights.1.weights_ref, bf16[144,768]{1,0:T(8,128)(2,1)} %get-tuple-element.120.refs_0_, bf16[144,768]{1,0:T(8,128)(2,1)} %collective-permute-done.5.refs_1_, bf16[144,768]{1,0:T(8,128)(2,1)} %collective-permute-done.3.refs_2_, ...), custom_call_target="tpu_custom_call" | custom-call | tf_op jit(solution)/shard_map/partial_sums/pallas_call | solution.py:148
  63.2 8.3 %pack_rows.8 = (bf16[144,1792]{1,0:T(8,128)(2,1)}, bf16[144,1792]{1,0:T(8,128)(2,1)}, bf16[144,1792]{1,0:T(8,128)(2,1)}, bf16[144,1792]{1,0:T(8,128)(2,1)}, bf16...) custom-call(s32[1]{0:T(128)} %bitcast.ctx_ref, ...), custom_call_target="tpu_custom_call" | custom-call | flops 999999995904 | tf_op jit(solution)/shard_map/pack_rows/pallas_call | solution.py:56
  82.0 14.4 %collective-permute-done.15.refs_6_ = bf16[144,1536]{1,0:T(8,128)(2,1)S(1)} collective-permute-done((bf16[144,1536]{1,0:T(8,128)(2,1)S(1)}, bf16[144,1536]{1,0:T(8,128)(2,1)S(1)}, u32[]{:S(2)}, u32[]{:S(2)}) %collective-permute-start.15) | collective-permute-done | bytes 442400 | tf_op jit(solution)/shard_map/ppermute | solution.py:34
  96.4 11.7 %collective-permute-done.16.refs_7_ = bf16[144,1536]{1,0:T(8,128)(2,1)S(1)} collective-permute-done((bf16[144,1536]{1,0:T(8,128)(2,1)S(1)}, bf16[144,1536]{1,0:T(8,128)(2,1)S(1)}, u32[]{:S(2)}, u32[]{:S(2)}) %collective-permute-start.16) | collective-permute-done | bytes 442400 | tf_op jit(solution)/shard_map/ppermute | solution.py:34
  108.8 6.1 %partial_sums.7 = bf16[512,1536]{1,0:T(8,128)(2,1)} custom-call(s32[1]{0:T(128)} %bitcast.1.side_ref, bf16[512,1152]{1,0:T(8,128)(2,1)} %combine_weights.1.weights_ref, bf16[144,1536]{1,0:T(8,128)(2,1)} %get-tuple-element.122.refs_0_, bf16[144,1536]{1,0:T(8,128)(2,1)} %copy-done.10, bf16[144,1536]{1,0:T(8,128)(2,1)} %copy-done.7, ...), custom_call_target="tpu_custom_call" | custom-call | tf_op jit(solution)/shard_map/partial_sums/pallas_call | solution.py:148
  119.1 11.9 %latent_attention.3 = bf16[768,128]{1,0:T(8,128)(2,1)} custom-call(s32[41]{0:T(128)} %pad_add_fusion.info, bf16[2048,192]{1,0:T(8,128)(2,1)} %copy.18.queries_ref, bf16[128,512]{1,0:T(8,128)(2,1)} %bitcast.40, bf16[512,128]{1,0:T(8,128)(2,1)} %bitcast.43, bf16[2048,576]{1,0:T(8,128)(2,1)} %copy-done, bf16[2048,576]{1,0:T(8,128)(2,1)} %all-gather.2.cloned.1.call-done.other_ref), custom_call_target="tpu_custom_call" | custom-call | flops 999999995904 | tf_op jit(solution)/shard_map/latent_attention/pallas_call | solution.py:260
  131.0 6.1 %pack_rows.9 = (bf16[144,1536]{1,0:T(8,128)(2,1)}, bf16[144,1536]{1,0:T(8,128)(2,1)}, bf16[144,1536]{1,0:T(8,128)(2,1)}, bf16[144,1536]{1,0:T(8,128)(2,1)}, bf16...) custom-call(s32[1]{0:T(128)} %bitcast.ctx_ref, ...), custom_call_target="tpu_custom_call" | custom-call | tf_op jit(solution)/shard_map/pack_rows/pallas_call | solution.py:56
  137.1 10.2 %collective-permute-start.27 = (bf16[144,1536]{1,0:T(8,128)(2,1)}, bf16[144,1536]{1,0:T(8,128)(2,1)S(1)}, u32[]{:S(2)}, u32[]{:S(2)}) collective-permute-start(bf16[144,1536]{1,0:T(8,128)(2,1)} %get-tuple-element.186), channel_id=1, source_target_pairs={{0,16},{1,17},{2,18},{3,19},{4,20},{5,21},{6,22},{7,23},{8,24},{9,... | collective-permute-start | bytes 1327112 | tf_op jit(solution)/shard_map/ppermute | solution.py:34
  147.3 4.2 %collective-permute-done.19.refs_3_ = bf16[144,1792]{1,0:T(8,128)(2,1)} collective-permute-done((bf16[144,1792]{1,0:T(8,128)(2,1)}, bf16[144,1792]{1,0:T(8,128)(2,1)}, u32[]{:S(2)}, u32[]{:S(2)}) %collective-permute-start.19) | collective-permute-done | bytes 516128 | tf_op jit(solution)/shard_map/ppermute | solution.py:34
  152.6 8.2 %partial_sums.8 = bf16[512,1792]{1,0:T(8,128)(2,1)} custom-call(s32[1]{0:T(128)} %bitcast.1.side_ref, bf16[512,1152]{1,0:T(8,128)(2,1)} %combine_weights.1.weights_ref, bf16[144,1792]{1,0:T(8,128)(2,1)} %get-tuple-element.138.refs_0_, bf16[144,1792]{1,0:T(8,128)(2,1)} %collective-permute-done.17.refs_1_, bf16[144,1792]{1,0:T(8,128)(2,1)} %copy-done.4, ...), custom_call_target="tpu_custom_call" | custom-call | tf_op jit(solution)/shard_map/partial_sums/pallas_call | solution.py:148
  165.8 14.1 %latent_attention.4 = bf16[768,128]{1,0:T(8,128)(2,1)} custom-call(s32[41]{0:T(128)} %pad_add_fusion.info, bf16[2048,192]{1,0:T(8,128)(2,1)} %copy.18.queries_ref, bf16[128,512]{1,0:T(8,128)(2,1)} %bitcast.41, bf16[512,128]{1,0:T(8,128)(2,1)} %bitcast.44, bf16[2048,576]{1,0:T(8,128)(2,1)} %copy-done, bf16[2048,576]{1,0:T(8,128)(2,1)} %all-gather.2.cloned.1.call-done.other_ref), custom_call_target="tpu_custom_call" | custom-call | flops 999999995904 | tf_op jit(solution)/shard_map/latent_attention/pallas_call | solution.py:260
  180.0 4.6 %pack_rows.10 = (bf16[144,1024]{1,0:T(8,128)(2,1)}, bf16[144,1024]{1,0:T(8,128)(2,1)}, bf16[144,1024]{1,0:T(8,128)(2,1)}, bf16[144,1024]{1,0:T(8,128)(2,1)}, bf1...) custom-call(s32[1]{0:T(128)} %bitcast.ctx_ref, ...), custom_call_target="tpu_custom_call" | custom-call | tf_op jit(solution)/shard_map/pack_rows/pallas_call | solution.py:56
  184.7 9.0 %collective-permute-done.26.refs_3_ = bf16[144,1536]{1,0:T(8,128)(2,1)} collective-permute-done((bf16[144,1536]{1,0:T(8,128)(2,1)}, bf16[144,1536]{1,0:T(8,128)(2,1)}, u32[]{:S(2)}, u32[]{:S(2)}) %collective-permute-start.26) | collective-permute-done | bytes 442400 | tf_op jit(solution)/shard_map/ppermute | solution.py:34
  194.8 6.1 %partial_sums.9 = bf16[512,1536]{1,0:T(8,128)(2,1)} custom-call(s32[1]{0:T(128)} %bitcast.1.side_ref, bf16[512,1152]{1,0:T(8,128)(2,1)} %combine_weights.1.weights_ref, bf16[144,1536]{1,0:T(8,128)(2,1)} %get-tuple-element.158.refs_0_, bf16[144,1536]{1,0:T(8,128)(2,1)} %collective-permute-done.24.refs_1_, bf16[144,1536]{1,0:T(8,128)(2,1)} %copy-done.9, ...), custom_call_target="tpu_custom_call" | custom-call | tf_op jit(solution)/shard_map/partial_sums/pallas_call | solution.py:148
  205.2 9.8 %latent_attention.5 = bf16[512,128]{1,0:T(8,128)(2,1)} custom-call(s32[41]{0:T(128)} %pad_add_fusion.info, bf16[2048,192]{1,0:T(8,128)(2,1)} %copy.18.queries_ref, bf16[128,512]{1,0:T(8,128)(2,1)} %bitcast.42, bf16[512,128]{1,0:T(8,128)(2,1)} %bitcast.45, bf16[2048,576]{1,0:T(8,128)(2,1)} %copy-done, bf16[2048,576]{1,0:T(8,128)(2,1)} %all-gather.2.cloned.1.call-done.other_ref), custom_call_target="tpu_custom_call" | custom-call | flops 999999995904 | tf_op jit(solution)/shard_map/latent_attention/pallas_call | solution.py:260
  218.4 5.1 %collective-permute-start.41 = (bf16[144,512]{1,0:T(8,128)(2,1)}, bf16[144,512]{1,0:T(8,128)(2,1)S(1)}, u32[]{:S(2)}, u32[]{:S(2)}) collective-permute-start(bf16[144,512]{1,0:T(8,128)(2,1)} %get-tuple-element.221), channel_id=1, source_target_pairs={{0,16},{1,17},{2,18},{3,19},{4,20},{5,21},{6,22},{7,23},{8,24},{9,... | collective-permute-start | bytes 442376 | tf_op jit(solution)/shard_map/ppermute | solution.py:34
  225.6 4.5 %partial_sums.10 = (bf16[256,1024]{1,0:T(8,128)(2,1)}, bf16[256,1024]{1,0:T(8,128)(2,1)}) custom-call(s32[1]{0:T(128)} %bitcast.1.side_ref, bf16[512,1152]{1,0:T(8,128)(2,1)} %combine_weights.1.weights_ref, bf16[144,1024]{1,0:T(8,128)(2,1)} %get-tuple-element.177.refs_0_, bf16[144,1024]{1,0:T(8,128)(2,1)} %collective-permute-done.31.refs_1_, ...), custom_call_target="tpu_custom_call" | custom-call | tf_op jit(solution)/shard_map/partial_sums/pallas_call | solution.py:148
  237.4 6.4 %collective-permute-done.40.refs_3_ = bf16[144,512]{1,0:T(8,128)(2,1)S(1)} collective-permute-done((bf16[144,512]{1,0:T(8,128)(2,1)S(1)}, bf16[144,512]{1,0:T(8,128)(2,1)S(1)}, u32[]{:S(2)}, u32[]{:S(2)}) %collective-permute-start.40) | collective-permute-done | bytes 147488 | tf_op jit(solution)/shard_map/ppermute | solution.py:34
  252.6 8.0 %collective-permute-done.47 = bf16[256,512]{1,0:T(8,128)(2,1)S(1)} collective-permute-done((bf16[256,512]{1,0:T(8,128)(2,1)}, bf16[256,512]{1,0:T(8,128)(2,1)S(1)}, u32[]{:S(2)}, u32[]{:S(2)}) %collective-permute-start.47) | collective-permute-done | bytes 262176 | tf_op jit(solution)/shard_map/ppermute | solution.py:34
  261.1 6.8 %collective-permute-done.46 = bf16[128,1024]{1,0:T(8,128)(2,1)S(1)} collective-permute-done((bf16[128,1024]{1,0:T(8,128)(2,1)S(1)}, bf16[128,1024]{1,0:T(8,128)(2,1)S(1)}, u32[]{:S(2)}, u32[]{:S(2)}) %collective-permute-start.46) | collective-permute-done | bytes 262176 | tf_op jit(solution)/shard_map/ppermute | solution.py:34
  (211 shorter events, 81.2 us)
Async XLA Ops:
  8.0 111.1 %reduce-scatter.5.cloned.1.call-start = ((), (), s32[]{:S(2)}) async-start(), calls=%async_computation.4 | async-start | bytes 983040 | tf_op jit(solution)/shard_map/reduce_scatter | solution.py:418
  28.2 31.8 %collective-permute-start.13 = (bf16[144,1536]{1,0:T(8,128)(2,1)}, bf16[144,1536]{1,0:T(8,128)(2,1)S(1)}, u32[]{:S(2)}, u32[]{:S(2)}) collective-permute-start(bf16[144,1536]{1,0:T(8,128)(2,1)} %get-tuple-element.147), channel_id=1, source_target_pairs={{0,16},{1,17},{2,18},{3,19},{4,20},{5,21},{6,22},{7,23},{8,24},{9,... | collective-permute-start | bytes 1327112 | tf_op jit(solution)/shard_map/ppermute | solution.py:34
  29.5 30.5 %collective-permute-start.11 = (bf16[144,1536]{1,0:T(8,128)(2,1)}, bf16[144,1536]{1,0:T(8,128)(2,1)S(1)}, u32[]{:S(2)}, u32[]{:S(2)}) collective-permute-start(bf16[144,1536]{1,0:T(8,128)(2,1)} %get-tuple-element.143), channel_id=1, source_target_pairs={{0,2},{1,3},{2,0},{3,1},{4,6},{5,7},{6,4},{7,5},{8,10},{9,11},{10,... | collective-permute-start | bytes 1327112 | tf_op jit(solution)/shard_map/ppermute | solution.py:34
  60.1 59.1 %all-gather.2.cloned.1.call-start = ((), (), s32[]{:S(2)}) async-start(), calls=%async_computation.5 | async-start | bytes 2949120 | tf_op jit(solution)/shard_map/all_gather | solution.py:343
  63.2 97.6 %reduce-scatter.7.cloned.1.call-start = ((), (), s32[]{:S(2)}) async-start(), calls=%async_computation.6 | async-start | bytes 1966080 | tf_op jit(solution)/shard_map/reduce_scatter | solution.py:418
  74.1 42.3 %collective-permute-start.20 = (bf16[144,1792]{1,0:T(8,128)(2,1)}, bf16[144,1792]{1,0:T(8,128)(2,1)S(1)}, u32[]{:S(2)}, u32[]{:S(2)}) collective-permute-start(bf16[144,1792]{1,0:T(8,128)(2,1)} %get-tuple-element.167), channel_id=1, source_target_pairs={{0,16},{1,17},{2,18},{3,19},{4,20},{5,21},{6,22},{7,23},{8,24},{9,... | collective-permute-start | bytes 1548296 | tf_op jit(solution)/shard_map/ppermute | solution.py:34
  74.8 42.6 %collective-permute-start.18 = (bf16[144,1792]{1,0:T(8,128)(2,1)}, bf16[144,1792]{1,0:T(8,128)(2,1)S(1)}, u32[]{:S(2)}, u32[]{:S(2)}) collective-permute-start(bf16[144,1792]{1,0:T(8,128)(2,1)} %get-tuple-element.163), channel_id=1, source_target_pairs={{0,2},{1,3},{2,0},{3,1},{4,6},{5,7},{6,4},{7,5},{8,10},{9,11},{10,... | collective-permute-start | bytes 1548296 | tf_op jit(solution)/shard_map/ppermute | solution.py:34
  79.4 28.6 %collective-permute-start.16 = (bf16[144,1536]{1,0:T(8,128)(2,1)S(1)}, bf16[144,1536]{1,0:T(8,128)(2,1)S(1)}, u32[]{:S(2)}, u32[]{:S(2)}) collective-permute-start(bf16[144,1536]{1,0:T(8,128)(2,1)S(1)} %copy-done.32), channel_id=1, source_target_pairs={{0,19},{1,18},{2,17},{3,16},{4,23},{5,22},{6,21},{7,20},{8,27},{9,... | collective-permute-start | bytes 1327112 | tf_op jit(solution)/shard_map/ppermute | solution.py:34
  81.5 55.6 %collective-permute-start.21 = (bf16[144,1792]{1,0:T(8,128)(2,1)}, bf16[144,1792]{1,0:T(8,128)(2,1)}, u32[]{:S(2)}, u32[]{:S(2)}) collective-permute-start(bf16[144,1792]{1,0:T(8,128)(2,1)} %get-tuple-element.169), channel_id=1, source_target_pairs={{0,17},{1,16},{2,19},{3,18},{4,21},{5,20},{6,23},{7,22},{8,25},{9,... | collective-permute-start | bytes 1548296 | tf_op jit(solution)/shard_map/ppermute | solution.py:34
  114.9 37.7 %collective-permute-start.17 = (bf16[144,1792]{1,0:T(8,128)(2,1)}, bf16[144,1792]{1,0:T(8,128)(2,1)}, u32[]{:S(2)}, u32[]{:S(2)}) collective-permute-start(bf16[144,1792]{1,0:T(8,128)(2,1)} %get-tuple-element.161), channel_id=1, source_target_pairs={{0,1},{1,0},{2,3},{3,2},{4,5},{5,4},{6,7},{7,6},{8,9},{9,8},{10,11... | collective-permute-start | bytes 1548296 | tf_op jit(solution)/shard_map/ppermute | solution.py:34
  114.9 36.6 %collective-permute-start.19 = (bf16[144,1792]{1,0:T(8,128)(2,1)}, bf16[144,1792]{1,0:T(8,128)(2,1)}, u32[]{:S(2)}, u32[]{:S(2)}) collective-permute-start(bf16[144,1792]{1,0:T(8,128)(2,1)} %get-tuple-element.165), channel_id=1, source_target_pairs={{0,3},{1,2},{2,1},{3,0},{4,7},{5,6},{6,5},{7,4},{8,11},{9,10},{10,... | collective-permute-start | bytes 1548296 | tf_op jit(solution)/shard_map/ppermute | solution.py:34
  116.4 36.2 %collective-permute-start.22 = (bf16[144,1792]{1,0:T(8,128)(2,1)}, bf16[144,1792]{1,0:T(8,128)(2,1)}, u32[]{:S(2)}, u32[]{:S(2)}) collective-permute-start(bf16[144,1792]{1,0:T(8,128)(2,1)} %get-tuple-element.171), channel_id=1, source_target_pairs={{0,18},{1,19},{2,16},{3,17},{4,22},{5,23},{6,20},{7,21},{8,26},{9,... | collective-permute-start | bytes 1548296 | tf_op jit(solution)/shard_map/ppermute | solution.py:34
  117.4 35.2 %collective-permute-start.23 = (bf16[144,1792]{1,0:T(8,128)(2,1)}, bf16[144,1792]{1,0:T(8,128)(2,1)}, u32[]{:S(2)}, u32[]{:S(2)}) collective-permute-start(bf16[144,1792]{1,0:T(8,128)(2,1)} %get-tuple-element.173), channel_id=1, source_target_pairs={{0,19},{1,18},{2,17},{3,16},{4,23},{5,22},{6,21},{7,20},{8,27},{9,... | collective-permute-start | bytes 1548296 | tf_op jit(solution)/shard_map/ppermute | solution.py:34
  119.0 86.1 %reduce-scatter.9.cloned.1.call-start = ((), (), s32[]{:S(2)}) async-start(), calls=%async_computation.7 | async-start | bytes 2293760 | tf_op jit(solution)/shard_map/reduce_scatter | solution.py:418
  137.1 25.7 %collective-permute-start.27 = (bf16[144,1536]{1,0:T(8,128)(2,1)}, bf16[144,1536]{1,0:T(8,128)(2,1)S(1)}, u32[]{:S(2)}, u32[]{:S(2)}) collective-permute-start(bf16[144,1536]{1,0:T(8,128)(2,1)} %get-tuple-element.186), channel_id=1, source_target_pairs={{0,16},{1,17},{2,18},{3,19},{4,20},{5,21},{6,22},{7,23},{8,24},{9,... | collective-permute-start | bytes 1327112 | tf_op jit(solution)/shard_map/ppermute | solution.py:34
  160.8 33.4 %collective-permute-start.24 = (bf16[144,1536]{1,0:T(8,128)(2,1)}, bf16[144,1536]{1,0:T(8,128)(2,1)}, u32[]{:S(2)}, u32[]{:S(2)}) collective-permute-start(bf16[144,1536]{1,0:T(8,128)(2,1)} %get-tuple-element.180), channel_id=1, source_target_pairs={{0,1},{1,0},{2,3},{3,2},{4,5},{5,4},{6,7},{7,6},{8,9},{9,8},{10,11... | collective-permute-start | bytes 1327112 | tf_op jit(solution)/shard_map/ppermute | solution.py:34
  161.3 23.3 %collective-permute-start.28 = (bf16[144,1536]{1,0:T(8,128)(2,1)}, bf16[144,1536]{1,0:T(8,128)(2,1)}, u32[]{:S(2)}, u32[]{:S(2)}) collective-permute-start(bf16[144,1536]{1,0:T(8,128)(2,1)} %get-tuple-element.188), channel_id=1, source_target_pairs={{0,17},{1,16},{2,19},{3,18},{4,21},{5,20},{6,23},{7,22},{8,25},{9,... | collective-permute-start | bytes 1327112 | tf_op jit(solution)/shard_map/ppermute | solution.py:34
  161.9 31.8 %collective-permute-start.26 = (bf16[144,1536]{1,0:T(8,128)(2,1)}, bf16[144,1536]{1,0:T(8,128)(2,1)}, u32[]{:S(2)}, u32[]{:S(2)}) collective-permute-start(bf16[144,1536]{1,0:T(8,128)(2,1)} %get-tuple-element.184), channel_id=1, source_target_pairs={{0,3},{1,2},{2,1},{3,0},{4,7},{5,6},{6,5},{7,4},{8,11},{9,10},{10,... | collective-permute-start | bytes 1327112 | tf_op jit(solution)/shard_map/ppermute | solution.py:34
  162.9 31.9 %collective-permute-start.29 = (bf16[144,1536]{1,0:T(8,128)(2,1)}, bf16[144,1536]{1,0:T(8,128)(2,1)}, u32[]{:S(2)}, u32[]{:S(2)}) collective-permute-start(bf16[144,1536]{1,0:T(8,128)(2,1)} %get-tuple-element.190), channel_id=1, source_target_pairs={{0,18},{1,19},{2,16},{3,17},{4,22},{5,23},{6,20},{7,21},{8,26},{9,... | collective-permute-start | bytes 1327112 | tf_op jit(solution)/shard_map/ppermute | solution.py:34
  164.3 84.2 %reduce-scatter.11.cloned.1.call-start = ((), (), s32[]{:S(2)}) async-start(), calls=%async_computation.8 | async-start | bytes 1966080 | tf_op jit(solution)/shard_map/reduce_scatter | solution.py:418
  164.5 30.3 %collective-permute-start.30 = (bf16[144,1536]{1,0:T(8,128)(2,1)}, bf16[144,1536]{1,0:T(8,128)(2,1)}, u32[]{:S(2)}, u32[]{:S(2)}) collective-permute-start(bf16[144,1536]{1,0:T(8,128)(2,1)} %get-tuple-element.192), channel_id=1, source_target_pairs={{0,19},{1,18},{2,17},{3,16},{4,23},{5,22},{6,21},{7,20},{8,27},{9,... | collective-permute-start | bytes 1327112 | tf_op jit(solution)/shard_map/ppermute | solution.py:34
  194.2 24.2 %collective-permute-start.35 = (bf16[144,1024]{1,0:T(8,128)(2,1)}, bf16[144,1024]{1,0:T(8,128)(2,1)}, u32[]{:S(2)}, u32[]{:S(2)}) collective-permute-start(bf16[144,1024]{1,0:T(8,128)(2,1)} %get-tuple-element.207), channel_id=1, source_target_pairs={{0,17},{1,16},{2,19},{3,18},{4,21},{5,20},{6,23},{7,22},{8,25},{9,... | collective-permute-start | bytes 884744 | tf_op jit(solution)/shard_map/ppermute | solution.py:34
  200.9 24.7 %collective-permute-start.31 = (bf16[144,1024]{1,0:T(8,128)(2,1)}, bf16[144,1024]{1,0:T(8,128)(2,1)}, u32[]{:S(2)}, u32[]{:S(2)}) collective-permute-start(bf16[144,1024]{1,0:T(8,128)(2,1)} %get-tuple-element.199), channel_id=1, source_target_pairs={{0,1},{1,0},{2,3},{3,2},{4,5},{5,4},{6,7},{7,6},{8,9},{9,8},{10,11... | collective-permute-start | bytes 884744 | tf_op jit(solution)/shard_map/ppermute | solution.py:34
  201.2 24.3 %collective-permute-start.36 = (bf16[144,1024]{1,0:T(8,128)(2,1)}, bf16[144,1024]{1,0:T(8,128)(2,1)}, u32[]{:S(2)}, u32[]{:S(2)}) collective-permute-start(bf16[144,1024]{1,0:T(8,128)(2,1)} %get-tuple-element.209), channel_id=1, source_target_pairs={{0,18},{1,19},{2,16},{3,17},{4,22},{5,23},{6,20},{7,21},{8,26},{9,... | collective-permute-start | bytes 884744 | tf_op jit(solution)/shard_map/ppermute | solution.py:34
  (71 other events, 812.1 us)
Sparse Core Ops, SparseCore 0:
  60.2 39.8 reduce-scatter.4
  119.1 34.9 reduce-scatter.6
  164.4 39.6 reduce-scatter.8
  206.3 34.4 reduce-scatter.10
Sparse Core Ops, SparseCore 1:
  63.2 43.7 all-gather.1

commit v3 on v2

--- a/solution.py
+++ b/solution.py
@@ -19,11 +19,12 @@
 SMALL = pl.CostEstimate(flops=0, bytes_accessed=0, transcendentals=0)
 LARGE = pl.CostEstimate(flops=10**12, bytes_accessed=0, transcendentals=0)
 
-STEPS = ((768, True), (1536, True), (1792, True), (1536, True), (1024, False), (512, False))
-QUERY_BLOCKS = (0, 3, 3, 2, 0, 0)
+STEPS = ((1024, True), (1536, True), (1536, True), (1536, True), (1024, False), (512, False))
+QUERY_BLOCKS = (0, 2, 3, 3, 0, 0)
+AHEAD = ((2, 3), (4,), (5,), (), (), ())
 LONG_PACKS = (1, 2)
 SENDS = (4, 2, 5, 3, 1, 6, 7)
-IN_FLIGHT = 5
+IN_FLIGHT = 6
 
 
 def after(value, *others):
@@ -35,7 +36,7 @@
 
 
 def tile_of(start, width):
-    for tile in (512, 256, 128):
+    for tile in (768, 512, 256, 128):
         if start % tile == 0 and width % tile == 0:
             return tile
     raise ValueError("columns")
@@ -408,21 +409,23 @@
             send(i + 1, SENDS[4:], *last)
         if QUERY_BLOCKS[i]:
             last = [attention_part(QUERY_BLOCKS[i], *last, pieces[i - 1])]
+        for j in AHEAD[i]:
+            packed[j] = pack_step(j, *last)
+            last = packed[j][:1]
         if i + 2 < steps:
-            packed[i + 2] = pack_step(i + 2, *last)
-            last = packed[i + 2][:1]
             send(i + 2, SENDS[:4])
         if not scattered:
             begin(i, *sums, bits[0])
         else:
             pieces[i] = lax.psum_scatter(
-                after(sums[0], held[i + 1][SENDS[0]], held[i + 1][SENDS[1]]),
+                after(sums[0], *[held[i + 1][part] for part in SENDS[: 0 if i else 4]]),
                 "exp",
                 scatter_dimension=0,
                 axis_index_groups=axis_groups,
                 tiled=True,
             )
-    pieces = [piece if piece is None else after(piece, *last) for piece in pieces]
+    final = max(i for i, (_, scattered) in enumerate(STEPS) if scattered)
+    pieces[final] = after(pieces[final], *last)
     while any(piece is None for piece in pieces):
         before = ()
         for i in range(steps):

time: 283 us -> 271 us (0.958)
  starting transfers between devices: 66.9 us -> 60.5 us
  Pallas kernels: 107 us -> 102 us
  waiting for transfers between devices: 77.8 us -> 74.5 us
    ppermute x49, starting transfers between devices: 66.5 us -> 60.2 us  [exchange(): return lax.ppermute(value, AXES, [(i, i ^ mask) for i in range(devices)])]
    ppermute x49, waiting for transfers between devices: 77.6 us -> 72.1 us  [exchange(): return lax.ppermute(value, AXES, [(i, i ^ mask) for i in range(devices)])]
    pallas_call x6, Pallas kernels: 32.9 us -> 29.2 us  [partial_sums(): pl.pallas_call(functools.partial(sums_kernel, tokens), grid_spec=pltpu.Pr...]
  transfers between devices with their start and end apart: 54 -> 54, of which waited for: 15 -> 18; matrix products, arithmetic and copies ran while one was open for 3% -> 4% of each run, Pallas kernels for 37% -> 36%
where the time goes in v3:
time: 271 us; the launch traced here: 267 us
  Pallas kernels  102 us (38%)
  waiting for transfers between devices  74.5 us (27%)
  starting transfers between devices  60.5 us (22%)
  between operations  15.9 us (6%)
  local copies, waits for them, and re-layouts  9.11 us (3%)
  other arithmetic  5 us (2%)
    ppermute x49, waiting for transfers between devices, exchange(): return lax.ppermute(value, AXES, [(i, i ^ mask) for i in range(devices)])  72.1 us
    ppermute x49, starting transfers between devices, exchange(): return lax.ppermute(value, AXES, [(i, i ^ mask) for i in range(devices)])  60.2 us
    pallas_call x3, Pallas kernels, attend(): pl.pallas_call(functools.partial(attention_kernel, 1.0 / math.sqrt(PLAIN_...  37.1 us
    pallas_call x6, Pallas kernels, pack(): pl.pallas_call(pack_kernel, grid_spec=pltpu.PrefetchScalarGridSpec(num_sc...  31.3 us
    pallas_call x6, Pallas kernels, partial_sums(): pl.pallas_call(functools.partial(sums_kernel, tokens), grid_spec=pltpu.Pr...  29.2 us
  transfers between devices with their start and end apart: 54, of which 18 were waited for; matrix products, arithmetic and copies ran while one was open for 4% of the time, Pallas kernels for 36%

profile of v3, /device:TPU:3, one launch (start us, length us, event | category | flops | bytes accessed | tf_op | source)
XLA Modules:
  0.0 266.9 jit_solution(10830327343624138284)
XLA Ops:
  9.1 4.6 %pack_rows.6 = (bf16[144,1024]{1,0:T(8,128)(2,1)}, bf16[144,1024]{1,0:T(8,128)(2,1)}, bf16[144,1024]{1,0:T(8,128)(2,1)}, bf16[144,1024]{1,0:T(8,128)(2,1)}, bf16...) custom-call(s32[1]{0:T(128)} %bitcast.ctx_ref, ...), custom_call_target="tpu_custom_call" | custom-call | tf_op jit(solution)/shard_map/pack_rows/pallas_call | solution.py:57
  19.1 6.1 %pack_rows.7 = (bf16[144,1536]{1,0:T(8,128)(2,1)}, bf16[144,1536]{1,0:T(8,128)(2,1)}, bf16[144,1536]{1,0:T(8,128)(2,1)}, bf16[144,1536]{1,0:T(8,128)(2,1)}, bf16...) custom-call(s32[1]{0:T(128)} %bitcast.ctx_ref, ...), custom_call_target="tpu_custom_call" | custom-call | flops 999999995904 | tf_op jit(solution)/shard_map/pack_rows/pallas_call | solution.py:57
  36.6 3.9 %collective-permute-start.12 = (bf16[144,1536]{1,0:T(8,128)(2,1)}, bf16[144,1536]{1,0:T(8,128)(2,1)}, u32[]{:S(2)}, u32[]{:S(2)}) collective-permute-start(bf16[144,1536]{1,0:T(8,128)(2,1)} %get-tuple-element.139), channel_id=1, source_target_pairs={{0,3},{1,2},{2,1},{3,0},{4,7},{5,6},{6,5},{7,4},{8,11},{9,10},{10,... | collective-permute-start | bytes 1327112 | tf_op jit(solution)/shard_map/ppermute | solution.py:35
  45.8 4.2 %combine_weights.1.weights_ref = bf16[512,1152]{1,0:T(8,128)(2,1)} custom-call(s32[1]{0:T(128)} %bitcast.2.me_ref, f32[4,16,128]{2,1,0:T(8,128)} %pad_maximum_fusion.1.routes_ref), custom_call_target="tpu_custom_call" | custom-call | tf_op jit(solution)/shard_map/combine_weights/pallas_call | solution.py:113
  50.0 18.8 %collective-permute-done.9.refs_7_ = bf16[144,1024]{1,0:T(8,128)(2,1)} collective-permute-done((bf16[144,1024]{1,0:T(8,128)(2,1)}, bf16[144,1024]{1,0:T(8,128)(2,1)}, u32[]{:S(2)}, u32[]{:S(2)}) %collective-permute-start.9) | collective-permute-done | bytes 294944 | tf_op jit(solution)/shard_map/ppermute | solution.py:35
  68.8 4.5 %partial_sums.6 = bf16[512,1024]{1,0:T(8,128)(2,1)} custom-call(s32[1]{0:T(128)} %bitcast.1.side_ref, bf16[512,1152]{1,0:T(8,128)(2,1)} %combine_weights.1.weights_ref, bf16[144,1024]{1,0:T(8,128)(2,1)} %get-tuple-element.113.refs_0_, bf16[144,1024]{1,0:T(8,128)(2,1)} %collective-permute-done.5.refs_1_, bf16[144,1024]{1,0:T(8,128)(2,1)} %collective-permute-done.3.refs_2_, ...), custom_call_target="tpu_custom_call" | custom-call | tf_op jit(solution)/shard_map/partial_sums/pallas_call | solution.py:149
  78.4 6.2 %pack_rows.8 = (bf16[144,1536]{1,0:T(8,128)(2,1)}, bf16[144,1536]{1,0:T(8,128)(2,1)}, bf16[144,1536]{1,0:T(8,128)(2,1)}, bf16[144,1536]{1,0:T(8,128)(2,1)}, bf16...) custom-call(s32[1]{0:T(128)} %bitcast.ctx_ref, ...), custom_call_target="tpu_custom_call" | custom-call | flops 999999995904 | tf_op jit(solution)/shard_map/pack_rows/pallas_call | solution.py:57
  84.6 6.5 %pack_rows.9 = (bf16[144,1536]{1,0:T(8,128)(2,1)}, bf16[144,1536]{1,0:T(8,128)(2,1)}, bf16[144,1536]{1,0:T(8,128)(2,1)}, bf16[144,1536]{1,0:T(8,128)(2,1)}, bf16...) custom-call(s32[1]{0:T(128)} %bitcast.ctx_ref, ...), custom_call_target="tpu_custom_call" | custom-call | tf_op jit(solution)/shard_map/pack_rows/pallas_call | solution.py:57
  95.0 3.8 %collective-permute-done.16.refs_7_ = bf16[144,1536]{1,0:T(8,128)(2,1)} collective-permute-done((bf16[144,1536]{1,0:T(8,128)(2,1)}, bf16[144,1536]{1,0:T(8,128)(2,1)}, u32[]{:S(2)}, u32[]{:S(2)}) %collective-permute-start.16) | collective-permute-done | bytes 442400 | tf_op jit(solution)/shard_map/ppermute | solution.py:35
  98.8 5.5 %partial_sums.7 = bf16[512,1536]{1,0:T(8,128)(2,1)} custom-call(s32[1]{0:T(128)} %bitcast.1.side_ref, bf16[512,1152]{1,0:T(8,128)(2,1)} %combine_weights.1.weights_ref, bf16[144,1536]{1,0:T(8,128)(2,1)} %get-tuple-element.115.refs_0_, bf16[144,1536]{1,0:T(8,128)(2,1)} %collective-permute-done.10.refs_1_, bf16[144,1536]{1,0:T(8,128)(2,1)} %collective-permute-done.11.refs_2_, ...), custom_call_target="tpu_custom_call" | custom-call | tf_op jit(solution)/shard_map/partial_sums/pallas_call | solution.py:149
  108.9 5.8 %collective-permute-done.20.refs_4_ = bf16[144,1536]{1,0:T(8,128)(2,1)S(1)} collective-permute-done((bf16[144,1536]{1,0:T(8,128)(2,1)S(1)}, bf16[144,1536]{1,0:T(8,128)(2,1)S(1)}, u32[]{:S(2)}, u32[]{:S(2)}) %collective-permute-start.20) | collective-permute-done | bytes 442400 | tf_op jit(solution)/shard_map/ppermute | solution.py:35
  114.7 3.5 %collective-permute-start.23 = (bf16[144,1536]{1,0:T(8,128)(2,1)}, bf16[144,1536]{1,0:T(8,128)(2,1)}, u32[]{:S(2)}, u32[]{:S(2)}) collective-permute-start(bf16[144,1536]{1,0:T(8,128)(2,1)} %get-tuple-element.167), channel_id=1, source_target_pairs={{0,19},{1,18},{2,17},{3,16},{4,23},{5,22},{6,21},{7,20},{8,27},{9,... | collective-permute-start | bytes 1327112 | tf_op jit(solution)/shard_map/ppermute | solution.py:35
  121.3 8.8 %latent_attention.3 = bf16[512,128]{1,0:T(8,128)(2,1)} custom-call(s32[41]{0:T(128)} %pad_add_fusion.info, bf16[2048,192]{1,0:T(8,128)(2,1)} %copy.18.queries_ref, bf16[128,512]{1,0:T(8,128)(2,1)} %bitcast.40, bf16[512,128]{1,0:T(8,128)(2,1)} %bitcast.43, bf16[2048,576]{1,0:T(8,128)(2,1)} %copy-done, bf16[2048,576]{1,0:T(8,128)(2,1)} %all-gather.2.cloned.1.call-done.other_ref), custom_call_target="tpu_custom_call" | custom-call | flops 999999995904 | tf_op jit(solution)/shard_map/latent_attention/pallas_call | solution.py:261
  130.2 4.6 %pack_rows.10 = (bf16[144,1024]{1,0:T(8,128)(2,1)}, bf16[144,1024]{1,0:T(8,128)(2,1)}, bf16[144,1024]{1,0:T(8,128)(2,1)}, bf16[144,1024]{1,0:T(8,128)(2,1)}, bf1...) custom-call(s32[1]{0:T(128)} %bitcast.ctx_ref, ...), custom_call_target="tpu_custom_call" | custom-call | tf_op jit(solution)/shard_map/pack_rows/pallas_call | solution.py:57
  137.0 7.9 %collective-permute-done.22.refs_6_ = bf16[144,1536]{1,0:T(8,128)(2,1)} collective-permute-done((bf16[144,1536]{1,0:T(8,128)(2,1)}, bf16[144,1536]{1,0:T(8,128)(2,1)}, u32[]{:S(2)}, u32[]{:S(2)}) %collective-permute-start.22) | collective-permute-done | bytes 442400 | tf_op jit(solution)/shard_map/ppermute | solution.py:35
  144.9 5.6 %partial_sums.8 = bf16[512,1536]{1,0:T(8,128)(2,1)} custom-call(s32[1]{0:T(128)} %bitcast.1.side_ref, bf16[512,1152]{1,0:T(8,128)(2,1)} %combine_weights.1.weights_ref, bf16[144,1536]{1,0:T(8,128)(2,1)} %get-tuple-element.130.refs_0_, bf16[144,1536]{1,0:T(8,128)(2,1)} %copy-done.7, bf16[144,1536]{1,0:T(8,128)(2,1)} %copy-done.4, ...), custom_call_target="tpu_custom_call" | custom-call | tf_op jit(solution)/shard_map/partial_sums/pallas_call | solution.py:149
  155.2 13.3 %latent_attention.4 = bf16[768,128]{1,0:T(8,128)(2,1)} custom-call(s32[41]{0:T(128)} %pad_add_fusion.info, bf16[2048,192]{1,0:T(8,128)(2,1)} %copy.18.queries_ref, bf16[128,512]{1,0:T(8,128)(2,1)} %bitcast.41, bf16[512,128]{1,0:T(8,128)(2,1)} %bitcast.44, bf16[2048,576]{1,0:T(8,128)(2,1)} %copy-done, bf16[2048,576]{1,0:T(8,128)(2,1)} %all-gather.2.cloned.1.call-done.other_ref), custom_call_target="tpu_custom_call" | custom-call | flops 999999995904 | tf_op jit(solution)/shard_map/latent_attention/pallas_call | solution.py:261
  171.9 5.9 %collective-permute-start.34 = (bf16[144,1024]{1,0:T(8,128)(2,1)S(1)}, bf16[144,1024]{1,0:T(8,128)(2,1)S(1)}, u32[]{:S(2)}, u32[]{:S(2)}) collective-permute-start(bf16[144,1024]{1,0:T(8,128)(2,1)S(1)} %copy-done.34), channel_id=1, source_target_pairs={{0,16},{1,17},{2,18},{3,19},{4,20},{5,21},{6,22},{7,23},{8,24},{9,... | collective-permute-start | bytes 884744 | tf_op jit(solution)/shard_map/ppermute | solution.py:35
  180.3 5.6 %partial_sums.9 = bf16[512,1536]{1,0:T(8,128)(2,1)} custom-call(s32[1]{0:T(128)} %bitcast.1.side_ref, bf16[512,1152]{1,0:T(8,128)(2,1)} %combine_weights.1.weights_ref, bf16[144,1536]{1,0:T(8,128)(2,1)} %get-tuple-element.132.refs_0_, bf16[144,1536]{1,0:T(8,128)(2,1)} %collective-permute-done.24.refs_1_, bf16[144,1536]{1,0:T(8,128)(2,1)} %collective-permute-done.25.refs_2_, ...), custom_call_target="tpu_custom_call" | custom-call | tf_op jit(solution)/shard_map/partial_sums/pallas_call | solution.py:149
  198.1 14.9 %latent_attention.5 = bf16[768,128]{1,0:T(8,128)(2,1)} custom-call(s32[41]{0:T(128)} %pad_add_fusion.info, bf16[2048,192]{1,0:T(8,128)(2,1)} %copy.18.queries_ref, bf16[128,512]{1,0:T(8,128)(2,1)} %bitcast.42, bf16[512,128]{1,0:T(8,128)(2,1)} %bitcast.45, bf16[2048,576]{1,0:T(8,128)(2,1)} %copy-done, bf16[2048,576]{1,0:T(8,128)(2,1)} %all-gather.2.cloned.1.call-done.other_ref), custom_call_target="tpu_custom_call" | custom-call | flops 999999995904 | tf_op jit(solution)/shard_map/latent_attention/pallas_call | solution.py:261
  213.3 4.7 %partial_sums.10 = (bf16[256,1024]{1,0:T(8,128)(2,1)}, bf16[256,1024]{1,0:T(8,128)(2,1)}) custom-call(s32[1]{0:T(128)} %bitcast.1.side_ref, bf16[512,1152]{1,0:T(8,128)(2,1)} %combine_weights.1.weights_ref, bf16[144,1024]{1,0:T(8,128)(2,1)} %get-tuple-element.152.refs_0_, bf16[144,1024]{1,0:T(8,128)(2,1)} %copy-done.15, bf16[144,1024]{1,0:T(8,128)(2,1)} %copy-done.13, ...), custom_call_target="tpu_custom_call" | custom-call | tf_op jit(solution)/shard_map/partial_sums/pallas_call | solution.py:149
  227.5 3.4 %collective-permute-done.43.refs_6_ = bf16[144,512]{1,0:T(8,128)(2,1)S(1)} collective-permute-done((bf16[144,512]{1,0:T(8,128)(2,1)S(1)}, bf16[144,512]{1,0:T(8,128)(2,1)S(1)}, u32[]{:S(2)}, u32[]{:S(2)}) %collective-permute-start.43) | collective-permute-done | bytes 147488 | tf_op jit(solution)/shard_map/ppermute | solution.py:35
  241.9 7.1 %collective-permute-done.47 = bf16[256,512]{1,0:T(8,128)(2,1)S(1)} collective-permute-done((bf16[256,512]{1,0:T(8,128)(2,1)}, bf16[256,512]{1,0:T(8,128)(2,1)S(1)}, u32[]{:S(2)}, u32[]{:S(2)}) %collective-permute-start.47) | collective-permute-done | bytes 262176 | tf_op jit(solution)/shard_map/ppermute | solution.py:35
  249.2 7.1 %collective-permute-done.46 = bf16[128,1024]{1,0:T(8,128)(2,1)S(1)} collective-permute-done((bf16[128,1024]{1,0:T(8,128)(2,1)S(1)}, bf16[128,1024]{1,0:T(8,128)(2,1)S(1)}, u32[]{:S(2)}, u32[]{:S(2)}) %collective-permute-start.46) | collective-permute-done | bytes 262176 | tf_op jit(solution)/shard_map/ppermute | solution.py:35
  (215 shorter events, 88.8 us)
Async XLA Ops:
  8.0 112.2 %reduce-scatter.5.cloned.1.call-start = ((), (), s32[]{:S(2)}) async-start(), calls=%async_computation.4 | async-start | bytes 1310720 | tf_op jit(solution)/shard_map/reduce_scatter | solution.py:420
  16.6 24.3 %collective-permute-start.8 = (bf16[144,1024]{1,0:T(8,128)(2,1)}, bf16[144,1024]{1,0:T(8,128)(2,1)}, u32[]{:S(2)}, u32[]{:S(2)}) collective-permute-start(bf16[144,1024]{1,0:T(8,128)(2,1)} %get-tuple-element.126), channel_id=1, source_target_pairs={{0,18},{1,19},{2,16},{3,17},{4,22},{5,23},{6,20},{7,21},{8,26},{9,... | collective-permute-start | bytes 884744 | tf_op jit(solution)/shard_map/ppermute | solution.py:35
  17.7 22.8 %collective-permute-start.6 = (bf16[144,1024]{1,0:T(8,128)(2,1)}, bf16[144,1024]{1,0:T(8,128)(2,1)}, u32[]{:S(2)}, u32[]{:S(2)}) collective-permute-start(bf16[144,1024]{1,0:T(8,128)(2,1)} %get-tuple-element.124), channel_id=1, source_target_pairs={{0,3},{1,2},{2,1},{3,0},{4,7},{5,6},{6,5},{7,4},{8,11},{9,10},{10,... | collective-permute-start | bytes 884744 | tf_op jit(solution)/shard_map/ppermute | solution.py:35
  36.6 36.7 %collective-permute-start.12 = (bf16[144,1536]{1,0:T(8,128)(2,1)}, bf16[144,1536]{1,0:T(8,128)(2,1)}, u32[]{:S(2)}, u32[]{:S(2)}) collective-permute-start(bf16[144,1536]{1,0:T(8,128)(2,1)} %get-tuple-element.139), channel_id=1, source_target_pairs={{0,3},{1,2},{2,1},{3,0},{4,7},{5,6},{6,5},{7,4},{8,11},{9,10},{10,... | collective-permute-start | bytes 1327112 | tf_op jit(solution)/shard_map/ppermute | solution.py:35
  40.5 32.9 %collective-permute-start.13 = (bf16[144,1536]{1,0:T(8,128)(2,1)}, bf16[144,1536]{1,0:T(8,128)(2,1)}, u32[]{:S(2)}, u32[]{:S(2)}) collective-permute-start(bf16[144,1536]{1,0:T(8,128)(2,1)} %get-tuple-element.141), channel_id=1, source_target_pairs={{0,16},{1,17},{2,18},{3,19},{4,20},{5,21},{6,22},{7,23},{8,24},{9,... | collective-permute-start | bytes 1327112 | tf_op jit(solution)/shard_map/ppermute | solution.py:35
  40.8 32.5 %collective-permute-start.11 = (bf16[144,1536]{1,0:T(8,128)(2,1)}, bf16[144,1536]{1,0:T(8,128)(2,1)}, u32[]{:S(2)}, u32[]{:S(2)}) collective-permute-start(bf16[144,1536]{1,0:T(8,128)(2,1)} %get-tuple-element.137), channel_id=1, source_target_pairs={{0,2},{1,3},{2,0},{3,1},{4,6},{5,7},{6,4},{7,5},{8,10},{9,11},{10,... | collective-permute-start | bytes 1327112 | tf_op jit(solution)/shard_map/ppermute | solution.py:35
  40.8 32.5 %collective-permute-start.14 = (bf16[144,1536]{1,0:T(8,128)(2,1)}, bf16[144,1536]{1,0:T(8,128)(2,1)}, u32[]{:S(2)}, u32[]{:S(2)}) collective-permute-start(bf16[144,1536]{1,0:T(8,128)(2,1)} %get-tuple-element.143), channel_id=1, source_target_pairs={{0,17},{1,16},{2,19},{3,18},{4,21},{5,20},{6,23},{7,22},{8,25},{9,... | collective-permute-start | bytes 1327112 | tf_op jit(solution)/shard_map/ppermute | solution.py:35
  43.1 25.8 %collective-permute-start.9 = (bf16[144,1024]{1,0:T(8,128)(2,1)}, bf16[144,1024]{1,0:T(8,128)(2,1)}, u32[]{:S(2)}, u32[]{:S(2)}) collective-permute-start(bf16[144,1024]{1,0:T(8,128)(2,1)} %get-tuple-element.128), channel_id=1, source_target_pairs={{0,19},{1,18},{2,17},{3,16},{4,23},{5,22},{6,21},{7,20},{8,27},{9,... | collective-permute-start | bytes 884744 | tf_op jit(solution)/shard_map/ppermute | solution.py:35
  73.4 47.9 %all-gather.2.cloned.1.call-start = ((), (), s32[]{:S(2)}) async-start(), calls=%async_computation.5 | async-start | bytes 2949120 | tf_op jit(solution)/shard_map/all_gather | solution.py:344
  76.7 78.2 %reduce-scatter.7.cloned.1.call-start = ((), (), s32[]{:S(2)}) async-start(), calls=%async_computation.6 | async-start | bytes 1966080 | tf_op jit(solution)/shard_map/reduce_scatter | solution.py:420
  93.5 24.8 %collective-permute-start.19 = (bf16[144,1536]{1,0:T(8,128)(2,1)S(1)}, bf16[144,1536]{1,0:T(8,128)(2,1)S(1)}, u32[]{:S(2)}, u32[]{:S(2)}) collective-permute-start(bf16[144,1536]{1,0:T(8,128)(2,1)S(1)} %copy-done.30), channel_id=1, source_target_pairs={{0,3},{1,2},{2,1},{3,0},{4,7},{5,6},{6,5},{7,4},{8,11},{9,10},{10,... | collective-permute-start | bytes 1327112 | tf_op jit(solution)/shard_map/ppermute | solution.py:35
  108.0 47.1 %collective-permute-start.25 = (bf16[144,1536]{1,0:T(8,128)(2,1)}, bf16[144,1536]{1,0:T(8,128)(2,1)}, u32[]{:S(2)}, u32[]{:S(2)}) collective-permute-start(bf16[144,1536]{1,0:T(8,128)(2,1)} %get-tuple-element.175), channel_id=1, source_target_pairs={{0,2},{1,3},{2,0},{3,1},{4,6},{5,7},{6,4},{7,5},{8,10},{9,11},{10,... | collective-permute-start | bytes 1327112 | tf_op jit(solution)/shard_map/ppermute | solution.py:35
  108.9 41.6 %collective-permute-start.27 = (bf16[144,1536]{1,0:T(8,128)(2,1)}, bf16[144,1536]{1,0:T(8,128)(2,1)}, u32[]{:S(2)}, u32[]{:S(2)}) collective-permute-start(bf16[144,1536]{1,0:T(8,128)(2,1)} %get-tuple-element.179), channel_id=1, source_target_pairs={{0,16},{1,17},{2,18},{3,19},{4,20},{5,21},{6,22},{7,23},{8,24},{9,... | collective-permute-start | bytes 1327112 | tf_op jit(solution)/shard_map/ppermute | solution.py:35
  118.2 79.9 %reduce-scatter.9.cloned.1.call-start = ((), (), s32[]{:S(2)}) async-start(), calls=%async_computation.7 | async-start | bytes 1966080 | tf_op jit(solution)/shard_map/reduce_scatter | solution.py:420
  118.3 26.6 %collective-permute-start.22 = (bf16[144,1536]{1,0:T(8,128)(2,1)}, bf16[144,1536]{1,0:T(8,128)(2,1)}, u32[]{:S(2)}, u32[]{:S(2)}) collective-permute-start(bf16[144,1536]{1,0:T(8,128)(2,1)} %get-tuple-element.165), channel_id=1, source_target_pairs={{0,18},{1,19},{2,16},{3,17},{4,22},{5,23},{6,20},{7,21},{8,26},{9,... | collective-permute-start | bytes 1327112 | tf_op jit(solution)/shard_map/ppermute | solution.py:35
  120.2 57.6 %collective-permute-start.28 = (bf16[144,1536]{1,0:T(8,128)(2,1)}, bf16[144,1536]{1,0:T(8,128)(2,1)}, u32[]{:S(2)}, u32[]{:S(2)}) collective-permute-start(bf16[144,1536]{1,0:T(8,128)(2,1)} %get-tuple-element.181), channel_id=1, source_target_pairs={{0,17},{1,16},{2,19},{3,18},{4,21},{5,20},{6,23},{7,22},{8,25},{9,... | collective-permute-start | bytes 1327112 | tf_op jit(solution)/shard_map/ppermute | solution.py:35
  137.0 34.9 %collective-permute-start.26 = (bf16[144,1536]{1,0:T(8,128)(2,1)}, bf16[144,1536]{1,0:T(8,128)(2,1)}, u32[]{:S(2)}, u32[]{:S(2)}) collective-permute-start(bf16[144,1536]{1,0:T(8,128)(2,1)} %get-tuple-element.177), channel_id=1, source_target_pairs={{0,3},{1,2},{2,1},{3,0},{4,7},{5,6},{6,5},{7,4},{8,11},{9,10},{10,... | collective-permute-start | bytes 1327112 | tf_op jit(solution)/shard_map/ppermute | solution.py:35
  150.5 28.7 %collective-permute-start.30 = (bf16[144,1536]{1,0:T(8,128)(2,1)}, bf16[144,1536]{1,0:T(8,128)(2,1)}, u32[]{:S(2)}, u32[]{:S(2)}) collective-permute-start(bf16[144,1536]{1,0:T(8,128)(2,1)} %get-tuple-element.185), channel_id=1, source_target_pairs={{0,19},{1,18},{2,17},{3,16},{4,23},{5,22},{6,21},{7,20},{8,27},{9,... | collective-permute-start | bytes 1327112 | tf_op jit(solution)/shard_map/ppermute | solution.py:35
  153.1 27.2 %collective-permute-start.29 = (bf16[144,1536]{1,0:T(8,128)(2,1)}, bf16[144,1536]{1,0:T(8,128)(2,1)}, u32[]{:S(2)}, u32[]{:S(2)}) collective-permute-start(bf16[144,1536]{1,0:T(8,128)(2,1)} %get-tuple-element.183), channel_id=1, source_target_pairs={{0,18},{1,19},{2,16},{3,17},{4,22},{5,23},{6,20},{7,21},{8,26},{9,... | collective-permute-start | bytes 1327112 | tf_op jit(solution)/shard_map/ppermute | solution.py:35
  154.9 81.8 %reduce-scatter.11.cloned.1.call-start = ((), (), s32[]{:S(2)}) async-start(), calls=%async_computation.8 | async-start | bytes 1966080 | tf_op jit(solution)/shard_map/reduce_scatter | solution.py:420
  155.1 23.1 %collective-permute-start.24 = (bf16[144,1536]{1,0:T(8,128)(2,1)}, bf16[144,1536]{1,0:T(8,128)(2,1)}, u32[]{:S(2)}, u32[]{:S(2)}) collective-permute-start(bf16[144,1536]{1,0:T(8,128)(2,1)} %get-tuple-element.173), channel_id=1, source_target_pairs={{0,1},{1,0},{2,3},{3,2},{4,5},{5,4},{6,7},{7,6},{8,9},{9,8},{10,11... | collective-permute-start | bytes 1327112 | tf_op jit(solution)/shard_map/ppermute | solution.py:35
  186.7 33.5 %collective-permute-start.41 = (bf16[144,512]{1,0:T(8,128)(2,1)}, bf16[144,512]{1,0:T(8,128)(2,1)}, u32[]{:S(2)}, u32[]{:S(2)}) collective-permute-start(bf16[144,512]{1,0:T(8,128)(2,1)} %get-tuple-element.211), channel_id=1, source_target_pairs={{0,16},{1,17},{2,18},{3,19},{4,20},{5,21},{6,22},{7,23},{8,24},{9,... | collective-permute-start | bytes 442376 | tf_op jit(solution)/shard_map/ppermute | solution.py:35
  192.2 30.1 %collective-permute-start.39 = (bf16[144,512]{1,0:T(8,128)(2,1)}, bf16[144,512]{1,0:T(8,128)(2,1)}, u32[]{:S(2)}, u32[]{:S(2)}) collective-permute-start(bf16[144,512]{1,0:T(8,128)(2,1)} %get-tuple-element.207), channel_id=1, source_target_pairs={{0,2},{1,3},{2,0},{3,1},{4,6},{5,7},{6,4},{7,5},{8,10},{9,11},{10,... | collective-permute-start | bytes 442376 | tf_op jit(solution)/shard_map/ppermute | solution.py:35
  196.2 27.2 %collective-permute-start.42 = (bf16[144,512]{1,0:T(8,128)(2,1)}, bf16[144,512]{1,0:T(8,128)(2,1)}, u32[]{:S(2)}, u32[]{:S(2)}) collective-permute-start(bf16[144,512]{1,0:T(8,128)(2,1)} %get-tuple-element.213), channel_id=1, source_target_pairs={{0,17},{1,16},{2,19},{3,18},{4,21},{5,20},{6,23},{7,22},{8,25},{9,... | collective-permute-start | bytes 442376 | tf_op jit(solution)/shard_map/ppermute | solution.py:35
  (73 other events, 931.9 us)
Sparse Core Ops, SparseCore 0:
  73.5 40.7 reduce-scatter.4
  118.3 34.5 reduce-scatter.6
  155.3 34.2 reduce-scatter.8
  194.2 42.4 reduce-scatter.10
Sparse Core Ops, SparseCore 1:
  76.7 44.5 all-gather.1

commit v4 on v3

--- a/solution.py
+++ b/solution.py
@@ -23,7 +23,7 @@
 QUERY_BLOCKS = (0, 2, 3, 3, 0, 0)
 AHEAD = ((2, 3), (4,), (5,), (), (), ())
 LONG_PACKS = (1, 2)
-SENDS = (4, 2, 5, 3, 1, 6, 7)
+SENDS = (4, 2, 5, 3, 1, 7, 6)
 IN_FLIGHT = 6
 
 

time: 271 us -> 268 us (0.989)
  starting transfers between devices: 60.5 us -> 53 us
  Pallas kernels: 102 us -> 108 us
    ppermute x49, starting transfers between devices: 60.2 us -> 52.6 us  [exchange(): return lax.ppermute(value, AXES, [(i, i ^ mask) for i in range(devices)])]
    ppermute x49, waiting for transfers between devices: 72.1 us -> 64.9 us  [exchange(): return lax.ppermute(value, AXES, [(i, i ^ mask) for i in range(devices)])]
    pallas_call x3, Pallas kernels: 37.1 us -> 43.1 us  [attend(): pl.pallas_call(functools.partial(attention_kernel, 1.0 / math.sqrt(PLAIN_...]
    reduce_scatter x4, waiting for transfers between devices: 1.23 us -> 7.02 us  [shards(): lax.psum_scatter(after(sums[0], *[held[i + 1][part] for part in SENDS[:0...]
  transfers between devices with their start and end apart: 54 -> 54, of which waited for: 18 -> 18; matrix products, arithmetic and copies ran while one was open for 4% -> 4% of each run, Pallas kernels for 36% -> 39%
where the time goes in v4:
time: 268 us; the launch traced here: 264 us
  Pallas kernels  108 us (40%)
  waiting for transfers between devices  73.7 us (28%)
  starting transfers between devices  53 us (20%)
  between operations  15.8 us (6%)
  local copies, waits for them, and re-layouts  9.14 us (3%)
  other arithmetic  5 us (2%)
    ppermute x49, waiting for transfers between devices, exchange(): return lax.ppermute(value, AXES, [(i, i ^ mask) for i in range(devices)])  64.9 us
    ppermute x49, starting transfers between devices, exchange(): return lax.ppermute(value, AXES, [(i, i ^ mask) for i in range(devices)])  52.6 us
    pallas_call x3, Pallas kernels, attend(): pl.pallas_call(functools.partial(attention_kernel, 1.0 / math.sqrt(PLAIN_...  43.1 us
    pallas_call x6, Pallas kernels, pack(): pl.pallas_call(pack_kernel, grid_spec=pltpu.PrefetchScalarGridSpec(num_sc...  31.2 us
    pallas_call x6, Pallas kernels, partial_sums(): pl.pallas_call(functools.partial(sums_kernel, tokens), grid_spec=pltpu.Pr...  29.1 us
    reduce_scatter x4, waiting for transfers between devices, shards(): lax.psum_scatter(after(sums[0], *[held[i + 1][part] for part in SENDS[:0...  7.02 us
    unnamed x91, local copies, waits for them, and re-layouts  5.38 us
  transfers between devices with their start and end apart: 54, of which 18 were waited for; matrix products, arithmetic and copies ran while one was open for 4% of the time, Pallas kernels for 39%

profile of v4, /device:TPU:3, one launch (start us, length us, event | category | flops | bytes accessed | tf_op | source)
XLA Modules:
  0.0 264.4 jit_solution(15474122303016604393)
XLA Ops:
  9.1 4.6 %pack_rows.6 = (bf16[144,1024]{1,0:T(8,128)(2,1)}, bf16[144,1024]{1,0:T(8,128)(2,1)}, bf16[144,1024]{1,0:T(8,128)(2,1)}, bf16[144,1024]{1,0:T(8,128)(2,1)}, bf16...) custom-call(s32[1]{0:T(128)} %bitcast.ctx_ref, ...), custom_call_target="tpu_custom_call" | custom-call | tf_op jit(solution)/shard_map/pack_rows/pallas_call | solution.py:57
  19.2 6.1 %pack_rows.7 = (bf16[144,1536]{1,0:T(8,128)(2,1)}, bf16[144,1536]{1,0:T(8,128)(2,1)}, bf16[144,1536]{1,0:T(8,128)(2,1)}, bf16[144,1536]{1,0:T(8,128)(2,1)}, bf16...) custom-call(s32[1]{0:T(128)} %bitcast.ctx_ref, ...), custom_call_target="tpu_custom_call" | custom-call | flops 999999995904 | tf_op jit(solution)/shard_map/pack_rows/pallas_call | solution.py:57
  36.6 4.5 %collective-permute-start.12 = (bf16[144,1536]{1,0:T(8,128)(2,1)}, bf16[144,1536]{1,0:T(8,128)(2,1)}, u32[]{:S(2)}, u32[]{:S(2)}) collective-permute-start(bf16[144,1536]{1,0:T(8,128)(2,1)} %get-tuple-element.139), channel_id=1, source_target_pairs={{0,3},{1,2},{2,1},{3,0},{4,7},{5,6},{6,5},{7,4},{8,11},{9,10},{10,... | collective-permute-start | bytes 1327112 | tf_op jit(solution)/shard_map/ppermute | solution.py:35
  44.8 4.2 %combine_weights.1.weights_ref = bf16[512,1152]{1,0:T(8,128)(2,1)} custom-call(s32[1]{0:T(128)} %bitcast.2.me_ref, f32[4,16,128]{2,1,0:T(8,128)} %pad_maximum_fusion.1.routes_ref), custom_call_target="tpu_custom_call" | custom-call | tf_op jit(solution)/shard_map/combine_weights/pallas_call | solution.py:113
  49.0 17.3 %collective-permute-done.8.refs_6_ = bf16[144,1024]{1,0:T(8,128)(2,1)} collective-permute-done((bf16[144,1024]{1,0:T(8,128)(2,1)}, bf16[144,1024]{1,0:T(8,128)(2,1)}, u32[]{:S(2)}, u32[]{:S(2)}) %collective-permute-start.8) | collective-permute-done | bytes 294944 | tf_op jit(solution)/shard_map/ppermute | solution.py:35
  66.3 4.5 %partial_sums.6 = bf16[512,1024]{1,0:T(8,128)(2,1)} custom-call(s32[1]{0:T(128)} %bitcast.1.side_ref, bf16[512,1152]{1,0:T(8,128)(2,1)} %combine_weights.1.weights_ref, bf16[144,1024]{1,0:T(8,128)(2,1)} %get-tuple-element.113.refs_0_, bf16[144,1024]{1,0:T(8,128)(2,1)} %collective-permute-done.5.refs_1_, bf16[144,1024]{1,0:T(8,128)(2,1)} %collective-permute-done.3.refs_2_, ...), custom_call_target="tpu_custom_call" | custom-call | tf_op jit(solution)/shard_map/partial_sums/pallas_call | solution.py:149
  78.4 6.2 %pack_rows.8 = (bf16[144,1536]{1,0:T(8,128)(2,1)}, bf16[144,1536]{1,0:T(8,128)(2,1)}, bf16[144,1536]{1,0:T(8,128)(2,1)}, bf16[144,1536]{1,0:T(8,128)(2,1)}, bf16...) custom-call(s32[1]{0:T(128)} %bitcast.ctx_ref, ...), custom_call_target="tpu_custom_call" | custom-call | flops 999999995904 | tf_op jit(solution)/shard_map/pack_rows/pallas_call | solution.py:57
  84.6 6.4 %pack_rows.9 = (bf16[144,1536]{1,0:T(8,128)(2,1)}, bf16[144,1536]{1,0:T(8,128)(2,1)}, bf16[144,1536]{1,0:T(8,128)(2,1)}, bf16[144,1536]{1,0:T(8,128)(2,1)}, bf16...) custom-call(s32[1]{0:T(128)} %bitcast.ctx_ref, ...), custom_call_target="tpu_custom_call" | custom-call | tf_op jit(solution)/shard_map/pack_rows/pallas_call | solution.py:57
  94.4 4.1 %collective-permute-done.15.refs_6_ = bf16[144,1536]{1,0:T(8,128)(2,1)} collective-permute-done((bf16[144,1536]{1,0:T(8,128)(2,1)}, bf16[144,1536]{1,0:T(8,128)(2,1)}, u32[]{:S(2)}, u32[]{:S(2)}) %collective-permute-start.15) | collective-permute-done | bytes 442400 | tf_op jit(solution)/shard_map/ppermute | solution.py:35
  98.5 5.6 %partial_sums.7 = bf16[512,1536]{1,0:T(8,128)(2,1)} custom-call(s32[1]{0:T(128)} %bitcast.1.side_ref, bf16[512,1152]{1,0:T(8,128)(2,1)} %combine_weights.1.weights_ref, bf16[144,1536]{1,0:T(8,128)(2,1)} %get-tuple-element.115.refs_0_, bf16[144,1536]{1,0:T(8,128)(2,1)} %collective-permute-done.10.refs_1_, bf16[144,1536]{1,0:T(8,128)(2,1)} %collective-permute-done.11.refs_2_, ...), custom_call_target="tpu_custom_call" | custom-call | tf_op jit(solution)/shard_map/partial_sums/pallas_call | solution.py:149
  108.7 6.7 %collective-permute-done.21.refs_5_ = bf16[144,1536]{1,0:T(8,128)(2,1)S(1)} collective-permute-done((bf16[144,1536]{1,0:T(8,128)(2,1)S(1)}, bf16[144,1536]{1,0:T(8,128)(2,1)S(1)}, u32[]{:S(2)}, u32[]{:S(2)}) %collective-permute-start.21) | collective-permute-done | bytes 442400 | tf_op jit(solution)/shard_map/ppermute | solution.py:35
  121.8 10.5 %latent_attention.3 = bf16[512,128]{1,0:T(8,128)(2,1)} custom-call(s32[41]{0:T(128)} %pad_add_fusion.info, bf16[2048,192]{1,0:T(8,128)(2,1)} %copy.18.queries_ref, bf16[128,512]{1,0:T(8,128)(2,1)} %bitcast.40, bf16[512,128]{1,0:T(8,128)(2,1)} %bitcast.43, bf16[2048,576]{1,0:T(8,128)(2,1)} %copy-done, bf16[2048,576]{1,0:T(8,128)(2,1)} %all-gather.2.cloned.1.call-done.other_ref), custom_call_target="tpu_custom_call" | custom-call | flops 999999995904 | tf_op jit(solution)/shard_map/latent_attention/pallas_call | solution.py:261
  132.4 4.6 %pack_rows.10 = (bf16[144,1024]{1,0:T(8,128)(2,1)}, bf16[144,1024]{1,0:T(8,128)(2,1)}, bf16[144,1024]{1,0:T(8,128)(2,1)}, bf16[144,1024]{1,0:T(8,128)(2,1)}, bf1...) custom-call(s32[1]{0:T(128)} %bitcast.ctx_ref, ...), custom_call_target="tpu_custom_call" | custom-call | tf_op jit(solution)/shard_map/pack_rows/pallas_call | solution.py:57
  138.5 5.6 %partial_sums.8 = bf16[512,1536]{1,0:T(8,128)(2,1)} custom-call(s32[1]{0:T(128)} %bitcast.1.side_ref, bf16[512,1152]{1,0:T(8,128)(2,1)} %combine_weights.1.weights_ref, bf16[144,1536]{1,0:T(8,128)(2,1)} %get-tuple-element.130.refs_0_, bf16[144,1536]{1,0:T(8,128)(2,1)} %copy-done.7, bf16[144,1536]{1,0:T(8,128)(2,1)} %copy-done.4, ...), custom_call_target="tpu_custom_call" | custom-call | tf_op jit(solution)/shard_map/partial_sums/pallas_call | solution.py:149
  146.6 7.0 %reduce-scatter.7.cloned.1.call-done = bf16[128,1536]{1,0:T(8,128)(2,1)} async-done(((bf16[512,1536]{1,0:T(8,128)(2,1)}), bf16[128,1536]{1,0:T(8,128)(2,1)}) %reduce-scatter.7.cloned.1.call-update) | async-done | bytes 393232 | tf_op jit(solution)/shard_map/reduce_scatter | solution.py:420
  154.7 12.6 %latent_attention.4 = bf16[768,128]{1,0:T(8,128)(2,1)} custom-call(s32[41]{0:T(128)} %pad_add_fusion.info, bf16[2048,192]{1,0:T(8,128)(2,1)} %copy.18.queries_ref, bf16[128,512]{1,0:T(8,128)(2,1)} %bitcast.41, bf16[512,128]{1,0:T(8,128)(2,1)} %bitcast.44, bf16[2048,576]{1,0:T(8,128)(2,1)} %copy-done, bf16[2048,576]{1,0:T(8,128)(2,1)} %all-gather.2.cloned.1.call-done.other_ref), custom_call_target="tpu_custom_call" | custom-call | flops 999999995904 | tf_op jit(solution)/shard_map/latent_attention/pallas_call | solution.py:261
  167.4 3.3 %pack_rows.11 = (bf16[144,512]{1,0:T(8,128)(2,1)}, bf16[144,512]{1,0:T(8,128)(2,1)}, bf16[144,512]{1,0:T(8,128)(2,1)}, bf16[144,512]{1,0:T(8,128)(2,1)}, bf16[14...) custom-call(s32[1]{0:T(128)} %bitcast.ctx_ref, ...), custom_call_target="tpu_custom_call" | custom-call | tf_op jit(solution)/shard_map/pack_rows/pallas_call | solution.py:57
  174.4 5.6 %partial_sums.9 = bf16[512,1536]{1,0:T(8,128)(2,1)} custom-call(s32[1]{0:T(128)} %bitcast.1.side_ref, bf16[512,1152]{1,0:T(8,128)(2,1)} %combine_weights.1.weights_ref, bf16[144,1536]{1,0:T(8,128)(2,1)} %get-tuple-element.132.refs_0_, bf16[144,1536]{1,0:T(8,128)(2,1)} %collective-permute-done.24.refs_1_, bf16[144,1536]{1,0:T(8,128)(2,1)} %collective-permute-done.25.refs_2_, ...), custom_call_target="tpu_custom_call" | custom-call | tf_op jit(solution)/shard_map/partial_sums/pallas_call | solution.py:149
  181.3 5.4 %collective-permute-done.35.refs_5_ = bf16[144,1024]{1,0:T(8,128)(2,1)S(1)} collective-permute-done((bf16[144,1024]{1,0:T(8,128)(2,1)S(1)}, bf16[144,1024]{1,0:T(8,128)(2,1)S(1)}, u32[]{:S(2)}, u32[]{:S(2)}) %collective-permute-start.35) | collective-permute-done | bytes 294944 | tf_op jit(solution)/shard_map/ppermute | solution.py:35
  190.8 20.0 %latent_attention.5 = bf16[768,128]{1,0:T(8,128)(2,1)} custom-call(s32[41]{0:T(128)} %pad_add_fusion.info, bf16[2048,192]{1,0:T(8,128)(2,1)} %copy.18.queries_ref, bf16[128,512]{1,0:T(8,128)(2,1)} %bitcast.42, bf16[512,128]{1,0:T(8,128)(2,1)} %bitcast.45, bf16[2048,576]{1,0:T(8,128)(2,1)} %copy-done, bf16[2048,576]{1,0:T(8,128)(2,1)} %all-gather.2.cloned.1.call-done.other_ref), custom_call_target="tpu_custom_call" | custom-call | flops 999999995904 | tf_op jit(solution)/shard_map/latent_attention/pallas_call | solution.py:261
  212.5 4.6 %partial_sums.10 = (bf16[256,1024]{1,0:T(8,128)(2,1)}, bf16[256,1024]{1,0:T(8,128)(2,1)}) custom-call(s32[1]{0:T(128)} %bitcast.1.side_ref, bf16[512,1152]{1,0:T(8,128)(2,1)} %combine_weights.1.weights_ref, bf16[144,1024]{1,0:T(8,128)(2,1)} %get-tuple-element.152.refs_0_, bf16[144,1024]{1,0:T(8,128)(2,1)} %copy-done.15, bf16[144,1024]{1,0:T(8,128)(2,1)} %copy-done.13, ...), custom_call_target="tpu_custom_call" | custom-call | tf_op jit(solution)/shard_map/partial_sums/pallas_call | solution.py:149
  222.3 3.5 %collective-permute-done.44.refs_7_ = bf16[144,512]{1,0:T(8,128)(2,1)S(1)} collective-permute-done((bf16[144,512]{1,0:T(8,128)(2,1)S(1)}, bf16[144,512]{1,0:T(8,128)(2,1)S(1)}, u32[]{:S(2)}, u32[]{:S(2)}) %collective-permute-start.44) | collective-permute-done | bytes 147488 | tf_op jit(solution)/shard_map/ppermute | solution.py:35
  238.9 6.3 %collective-permute-done.47 = bf16[256,512]{1,0:T(8,128)(2,1)S(1)} collective-permute-done((bf16[256,512]{1,0:T(8,128)(2,1)}, bf16[256,512]{1,0:T(8,128)(2,1)S(1)}, u32[]{:S(2)}, u32[]{:S(2)}) %collective-permute-start.47) | collective-permute-done | bytes 262176 | tf_op jit(solution)/shard_map/ppermute | solution.py:35
  245.4 8.4 %collective-permute-done.46 = bf16[128,1024]{1,0:T(8,128)(2,1)S(1)} collective-permute-done((bf16[128,1024]{1,0:T(8,128)(2,1)S(1)}, bf16[128,1024]{1,0:T(8,128)(2,1)S(1)}, u32[]{:S(2)}, u32[]{:S(2)}) %collective-permute-start.46) | collective-permute-done | bytes 262176 | tf_op jit(solution)/shard_map/ppermute | solution.py:35
  (215 shorter events, 80.9 us)
Async XLA Ops:
  8.0 112.1 %reduce-scatter.5.cloned.1.call-start = ((), (), s32[]{:S(2)}) async-start(), calls=%async_computation.4 | async-start | bytes 1310720 | tf_op jit(solution)/shard_map/reduce_scatter | solution.py:420
  16.5 24.6 %collective-permute-start.9 = (bf16[144,1024]{1,0:T(8,128)(2,1)}, bf16[144,1024]{1,0:T(8,128)(2,1)}, u32[]{:S(2)}, u32[]{:S(2)}) collective-permute-start(bf16[144,1024]{1,0:T(8,128)(2,1)} %get-tuple-element.128), channel_id=1, source_target_pairs={{0,19},{1,18},{2,17},{3,16},{4,23},{5,22},{6,21},{7,20},{8,27},{9,... | collective-permute-start | bytes 884744 | tf_op jit(solution)/shard_map/ppermute | solution.py:35
  36.6 34.3 %collective-permute-start.13 = (bf16[144,1536]{1,0:T(8,128)(2,1)}, bf16[144,1536]{1,0:T(8,128)(2,1)}, u32[]{:S(2)}, u32[]{:S(2)}) collective-permute-start(bf16[144,1536]{1,0:T(8,128)(2,1)} %get-tuple-element.141), channel_id=1, source_target_pairs={{0,16},{1,17},{2,18},{3,19},{4,20},{5,21},{6,22},{7,23},{8,24},{9,... | collective-permute-start | bytes 1327112 | tf_op jit(solution)/shard_map/ppermute | solution.py:35
  36.6 34.3 %collective-permute-start.12 = (bf16[144,1536]{1,0:T(8,128)(2,1)}, bf16[144,1536]{1,0:T(8,128)(2,1)}, u32[]{:S(2)}, u32[]{:S(2)}) collective-permute-start(bf16[144,1536]{1,0:T(8,128)(2,1)} %get-tuple-element.139), channel_id=1, source_target_pairs={{0,3},{1,2},{2,1},{3,0},{4,7},{5,6},{6,5},{7,4},{8,11},{9,10},{10,... | collective-permute-start | bytes 1327112 | tf_op jit(solution)/shard_map/ppermute | solution.py:35
  41.1 29.8 %collective-permute-start.11 = (bf16[144,1536]{1,0:T(8,128)(2,1)}, bf16[144,1536]{1,0:T(8,128)(2,1)}, u32[]{:S(2)}, u32[]{:S(2)}) collective-permute-start(bf16[144,1536]{1,0:T(8,128)(2,1)} %get-tuple-element.137), channel_id=1, source_target_pairs={{0,2},{1,3},{2,0},{3,1},{4,6},{5,7},{6,4},{7,5},{8,10},{9,11},{10,... | collective-permute-start | bytes 1327112 | tf_op jit(solution)/shard_map/ppermute | solution.py:35
  41.1 29.8 %collective-permute-start.14 = (bf16[144,1536]{1,0:T(8,128)(2,1)}, bf16[144,1536]{1,0:T(8,128)(2,1)}, u32[]{:S(2)}, u32[]{:S(2)}) collective-permute-start(bf16[144,1536]{1,0:T(8,128)(2,1)} %get-tuple-element.143), channel_id=1, source_target_pairs={{0,17},{1,16},{2,19},{3,18},{4,21},{5,20},{6,23},{7,22},{8,25},{9,... | collective-permute-start | bytes 1327112 | tf_op jit(solution)/shard_map/ppermute | solution.py:35
  70.9 50.9 %all-gather.2.cloned.1.call-start = ((), (), s32[]{:S(2)}) async-start(), calls=%async_computation.5 | async-start | bytes 2949120 | tf_op jit(solution)/shard_map/all_gather | solution.py:344
  76.1 77.5 %reduce-scatter.7.cloned.1.call-start = ((), (), s32[]{:S(2)}) async-start(), calls=%async_computation.6 | async-start | bytes 1966080 | tf_op jit(solution)/shard_map/reduce_scatter | solution.py:420
  91.6 23.8 %collective-permute-start.21 = (bf16[144,1536]{1,0:T(8,128)(2,1)S(1)}, bf16[144,1536]{1,0:T(8,128)(2,1)S(1)}, u32[]{:S(2)}, u32[]{:S(2)}) collective-permute-start(bf16[144,1536]{1,0:T(8,128)(2,1)S(1)} %copy-done.31), channel_id=1, source_target_pairs={{0,17},{1,16},{2,19},{3,18},{4,21},{5,20},{6,23},{7,22},{8,25},{9,... | collective-permute-start | bytes 1327112 | tf_op jit(solution)/shard_map/ppermute | solution.py:35
  94.0 23.5 %collective-permute-start.19 = (bf16[144,1536]{1,0:T(8,128)(2,1)S(1)}, bf16[144,1536]{1,0:T(8,128)(2,1)S(1)}, u32[]{:S(2)}, u32[]{:S(2)}) collective-permute-start(bf16[144,1536]{1,0:T(8,128)(2,1)S(1)} %copy-done.30), channel_id=1, source_target_pairs={{0,3},{1,2},{2,1},{3,0},{4,7},{5,6},{6,5},{7,4},{8,11},{9,10},{10,... | collective-permute-start | bytes 1327112 | tf_op jit(solution)/shard_map/ppermute | solution.py:35
  107.3 29.7 %collective-permute-start.23 = (bf16[144,1536]{1,0:T(8,128)(2,1)}, bf16[144,1536]{1,0:T(8,128)(2,1)}, u32[]{:S(2)}, u32[]{:S(2)}) collective-permute-start(bf16[144,1536]{1,0:T(8,128)(2,1)} %get-tuple-element.167), channel_id=1, source_target_pairs={{0,19},{1,18},{2,17},{3,16},{4,23},{5,22},{6,21},{7,20},{8,27},{9,... | collective-permute-start | bytes 1327112 | tf_op jit(solution)/shard_map/ppermute | solution.py:35
  107.3 31.2 %collective-permute-start.22 = (bf16[144,1536]{1,0:T(8,128)(2,1)}, bf16[144,1536]{1,0:T(8,128)(2,1)}, u32[]{:S(2)}, u32[]{:S(2)}) collective-permute-start(bf16[144,1536]{1,0:T(8,128)(2,1)} %get-tuple-element.165), channel_id=1, source_target_pairs={{0,18},{1,19},{2,16},{3,17},{4,22},{5,23},{6,20},{7,21},{8,26},{9,... | collective-permute-start | bytes 1327112 | tf_op jit(solution)/shard_map/ppermute | solution.py:35
  115.4 29.9 %collective-permute-start.27 = (bf16[144,1536]{1,0:T(8,128)(2,1)}, bf16[144,1536]{1,0:T(8,128)(2,1)}, u32[]{:S(2)}, u32[]{:S(2)}) collective-permute-start(bf16[144,1536]{1,0:T(8,128)(2,1)} %get-tuple-element.179), channel_id=1, source_target_pairs={{0,16},{1,17},{2,18},{3,19},{4,20},{5,21},{6,22},{7,23},{8,24},{9,... | collective-permute-start | bytes 1327112 | tf_op jit(solution)/shard_map/ppermute | solution.py:35
  117.2 73.6 %reduce-scatter.9.cloned.1.call-start = ((), (), s32[]{:S(2)}) async-start(), calls=%async_computation.7 | async-start | bytes 1966080 | tf_op jit(solution)/shard_map/reduce_scatter | solution.py:420
  117.5 36.4 %collective-permute-start.25 = (bf16[144,1536]{1,0:T(8,128)(2,1)}, bf16[144,1536]{1,0:T(8,128)(2,1)}, u32[]{:S(2)}, u32[]{:S(2)}) collective-permute-start(bf16[144,1536]{1,0:T(8,128)(2,1)} %get-tuple-element.175), channel_id=1, source_target_pairs={{0,2},{1,3},{2,0},{3,1},{4,6},{5,7},{6,4},{7,5},{8,10},{9,11},{10,... | collective-permute-start | bytes 1327112 | tf_op jit(solution)/shard_map/ppermute | solution.py:35
  117.9 53.0 %collective-permute-start.28 = (bf16[144,1536]{1,0:T(8,128)(2,1)}, bf16[144,1536]{1,0:T(8,128)(2,1)}, u32[]{:S(2)}, u32[]{:S(2)}) collective-permute-start(bf16[144,1536]{1,0:T(8,128)(2,1)} %get-tuple-element.181), channel_id=1, source_target_pairs={{0,17},{1,16},{2,19},{3,18},{4,21},{5,20},{6,23},{7,22},{8,25},{9,... | collective-permute-start | bytes 1327112 | tf_op jit(solution)/shard_map/ppermute | solution.py:35
  137.0 33.7 %collective-permute-start.26 = (bf16[144,1536]{1,0:T(8,128)(2,1)}, bf16[144,1536]{1,0:T(8,128)(2,1)}, u32[]{:S(2)}, u32[]{:S(2)}) collective-permute-start(bf16[144,1536]{1,0:T(8,128)(2,1)} %get-tuple-element.177), channel_id=1, source_target_pairs={{0,3},{1,2},{2,1},{3,0},{4,7},{5,6},{6,5},{7,4},{8,11},{9,10},{10,... | collective-permute-start | bytes 1327112 | tf_op jit(solution)/shard_map/ppermute | solution.py:35
  144.1 29.6 %collective-permute-start.30 = (bf16[144,1536]{1,0:T(8,128)(2,1)}, bf16[144,1536]{1,0:T(8,128)(2,1)}, u32[]{:S(2)}, u32[]{:S(2)}) collective-permute-start(bf16[144,1536]{1,0:T(8,128)(2,1)} %get-tuple-element.185), channel_id=1, source_target_pairs={{0,19},{1,18},{2,17},{3,16},{4,23},{5,22},{6,21},{7,20},{8,27},{9,... | collective-permute-start | bytes 1327112 | tf_op jit(solution)/shard_map/ppermute | solution.py:35
  145.3 29.1 %collective-permute-start.29 = (bf16[144,1536]{1,0:T(8,128)(2,1)}, bf16[144,1536]{1,0:T(8,128)(2,1)}, u32[]{:S(2)}, u32[]{:S(2)}) collective-permute-start(bf16[144,1536]{1,0:T(8,128)(2,1)} %get-tuple-element.183), channel_id=1, source_target_pairs={{0,18},{1,19},{2,16},{3,17},{4,22},{5,23},{6,20},{7,21},{8,26},{9,... | collective-permute-start | bytes 1327112 | tf_op jit(solution)/shard_map/ppermute | solution.py:35
  153.6 79.7 %reduce-scatter.11.cloned.1.call-start = ((), (), s32[]{:S(2)}) async-start(), calls=%async_computation.8 | async-start | bytes 1966080 | tf_op jit(solution)/shard_map/reduce_scatter | solution.py:420
  181.3 37.1 %collective-permute-start.41 = (bf16[144,512]{1,0:T(8,128)(2,1)}, bf16[144,512]{1,0:T(8,128)(2,1)}, u32[]{:S(2)}, u32[]{:S(2)}) collective-permute-start(bf16[144,512]{1,0:T(8,128)(2,1)} %get-tuple-element.211), channel_id=1, source_target_pairs={{0,16},{1,17},{2,18},{3,19},{4,20},{5,21},{6,22},{7,23},{8,24},{9,... | collective-permute-start | bytes 442376 | tf_op jit(solution)/shard_map/ppermute | solution.py:35
  186.7 31.8 %collective-permute-start.39 = (bf16[144,512]{1,0:T(8,128)(2,1)}, bf16[144,512]{1,0:T(8,128)(2,1)}, u32[]{:S(2)}, u32[]{:S(2)}) collective-permute-start(bf16[144,512]{1,0:T(8,128)(2,1)} %get-tuple-element.207), channel_id=1, source_target_pairs={{0,2},{1,3},{2,0},{3,1},{4,6},{5,7},{6,4},{7,5},{8,10},{9,11},{10,... | collective-permute-start | bytes 442376 | tf_op jit(solution)/shard_map/ppermute | solution.py:35
  188.3 24.2 %collective-permute-start.36 = (bf16[144,1024]{1,0:T(8,128)(2,1)}, bf16[144,1024]{1,0:T(8,128)(2,1)}, u32[]{:S(2)}, u32[]{:S(2)}) collective-permute-start(bf16[144,1024]{1,0:T(8,128)(2,1)} %get-tuple-element.199), channel_id=1, source_target_pairs={{0,18},{1,19},{2,16},{3,17},{4,22},{5,23},{6,20},{7,21},{8,26},{9,... | collective-permute-start | bytes 884744 | tf_op jit(solution)/shard_map/ppermute | solution.py:35
  190.1 31.2 %collective-permute-start.42 = (bf16[144,512]{1,0:T(8,128)(2,1)}, bf16[144,512]{1,0:T(8,128)(2,1)}, u32[]{:S(2)}, u32[]{:S(2)}) collective-permute-start(bf16[144,512]{1,0:T(8,128)(2,1)} %get-tuple-element.213), channel_id=1, source_target_pairs={{0,17},{1,16},{2,19},{3,18},{4,21},{5,20},{6,23},{7,22},{8,25},{9,... | collective-permute-start | bytes 442376 | tf_op jit(solution)/shard_map/ppermute | solution.py:35
  (73 other events, 945.6 us)
Sparse Core Ops, SparseCore 0:
  71.0 43.7 reduce-scatter.4
  117.8 35.7 reduce-scatter.6
  156.0 34.2 reduce-scatter.8
  192.6 38.9 reduce-scatter.10
Sparse Core Ops, SparseCore 1:
  76.2 45.6 all-gather.1
